TPU v7x, 128 devices: a whole 4x4x4 slice. The times are simulated.
128 devices in a mesh: gx: 8 (over z, core), gy: 16 (over y, x).
Axes of the slice: x: 4, y: 4, z: 4, core: 2. Of those that a mesh axis runs over, the one named last changes fastest.
Arguments:
- depth: float32 [2048, 16384], P('gx', 'gy'), may hold values from 2 to 4
- momentum_x: float32 [2048, 16384], P('gx', 'gy'), may hold values from -3 to 3
- momentum_y: float32 [2048, 16384], P('gx', 'gy'), may hold values from -3 to 3
- bed: float32 [2048, 16384], P('gx', 'gy'), may hold values from 0 to 1
- open_cell: int32 [2048, 16384], P('gx', 'gy'), may hold values 0 or 1
- send_strip: int32 [128, 128, 16], P(('gx', 'gy')), may hold values from -1 to 2047, as said below
- inlet_slot: int32 [2048, 128], P(('gx', 'gy')), may hold values from -1 to 2047, as said below
- inlet_section: int32 [2048, 128], P(('gx', 'gy')), may hold values from 0 to 511
- inlet_coef: float32 [2048, 128], P(('gx', 'gy')), may hold values from 0.1 to 1
- sewer_head: float32 [2048, 512], P(('gx', 'gy')), may hold values from -4 to 4
- conveyance: float32 [2048, 512], P(('gx', 'gy')), may hold values from 0.1 to 1
Outputs:
- depth_out: float32 [2048, 16384], P('gx', 'gy')
- momentum_x_out: float32 [2048, 16384], P('gx', 'gy')
- momentum_y_out: float32 [2048, 16384], P('gx', 'gy')
- sewer_out: float32 [2048, 512], P(('gx', 'gy'))
Inputs may be any that keep to these rules, and one draw needn't show every extreme that they name: Entry [s, d, k] is a strip of tile s, or -1 for an empty slot; used slots come first. No strip of a tile appears twice in send_strip[s]. Each tile sends at most 16 strips to one device, exactly 16 to some device in every column d, and one device receives 16 strips from every tile. `inlet_slot`: over the 16 lines of one device, each used slot s * 16 + k of what that device receives appears exactly once; every other entry is -1.
All inputs are finite; a program needn't handle non-finite values. No bound on the sum of `open_cell` on one device may be relied on, other than what follows from the above.
Results may differ from a plain program's by a relative error of at most 0.00012.
Values sent between devices are 32-bit elements; how exact they have to be, the bound alone decides.
A program may use at most 128 MiB of HBM per device.

v0:
```python
import functools
import math

import jax
import jax.numpy as jnp
from jax import lax
from jax.experimental import pallas as pl
from jax.experimental.pallas import tpu as pltpu
from jax.sharding import PartitionSpec as P

SUBSTEPS = 8
GRAVITY = 9.81
DT = 0.02
SEWER_DT = 0.5
AREA = 256.0
HALF_DT = 0.5 * DT
ROOT_G = math.sqrt(GRAVITY)
HALF_G = 0.5 * GRAVITY
SLOPE = 0.5 * GRAVITY * DT
NGX = 8
NGY = 16
ROWS = 256
UNROLL = 8
F32 = jnp.float32
BF16 = jnp.bfloat16
I32 = jnp.int32
NT = (((1,), (1,)), ((), ()))


def thirds(x):
    a = x.astype(BF16)
    rest = x - a.astype(F32)
    b = rest.astype(BF16)
    c = (rest - b.astype(F32)).astype(BF16)
    return a, b, c


def lanes_at(row, idx):
    return jnp.take_along_axis(row, idx, axis=1, mode="promise_in_bounds")


def prim(h, hu, hv, om):
    hs = h + om
    y = lax.rsqrt(hs)
    inv = y * y
    u = hu * inv
    v = hv * inv
    c = (ROOT_G * hs) * y
    p = HALF_G * h * h
    return dict(
        h=h,
        hu=hu,
        hv=hv,
        uu=hu * u + p,
        uv=hu * v,
        vv=hv * v + p,
        sx=jnp.abs(u) + c,
        sy=jnp.abs(v) + c,
    )


def face_x(wall, l, r):
    a = jnp.maximum(l["sx"], r["sx"])
    return (
        wall * ((l["hu"] + r["hu"]) - a * (r["h"] - l["h"])),
        wall * ((l["uu"] + r["uu"]) - a * (r["hu"] - l["hu"])),
        wall * ((l["uv"] + r["uv"]) - a * (r["hv"] - l["hv"])),
    )


def face_y(wall, l, r):
    a = jnp.maximum(l["sy"], r["sy"])
    return (
        wall * ((l["hv"] + r["hv"]) - a * (r["h"] - l["h"])),
        wall * ((l["uv"] + r["uv"]) - a * (r["hu"] - l["hu"])),
        wall * ((l["vv"] + r["vv"]) - a * (r["hv"] - l["hv"])),
    )


def kernel(
    depth, mom_x, mom_y, bed, cells, strips, slots, sections, coefs, heads, conv,
    out_h, out_hu, out_hv, out_sewer,
    h0, hu0, hv0, z0, m0, level, h1, hu1, hv1, h2, hu2, hv2,
    om_s, wx_s, wy_s, sx_s, sy_s,
    onehot, msg, mid, mid_t, got, cpt,
    row_snd1, row_rcv1, row_snd2, row_rcv2, col_snd1, col_rcv1, col_snd2, col_rcv2,
    inflow_s,
    in_sem, out_sem, p1_send, p1_recv, p2_send, p2_recv, halo_send, halo_recv,
):
    gx = lax.axis_index("gx")
    gy = lax.axis_index("gy")

    def gx_peer(i):
        return {"gx": lax.rem(gx + i, NGX)}

    def gy_peer(i):
        return {"gy": lax.rem(gy + i, NGY)}

    pairs = ((depth, h0), (bed, z0), (cells, m0), (mom_x, hu0), (mom_y, hv0))

    def load(f, j):
        src, dst = pairs[f]
        return pltpu.make_async_copy(
            src.at[:, pl.ds(128 * j, 128)], dst.at[pl.ds(0, ROWS), j, :], in_sem.at[f, j]
        )

    for f in range(5):
        for j in range(8):
            load(f, j).start()

    barrier = pltpu.get_barrier_semaphore()
    for i in range(1, NGX):
        pl.semaphore_signal(barrier, inc=1, device_id=gx_peer(i), device_id_type=pl.DeviceIdType.MESH)
    for i in range(1, NGY):
        pl.semaphore_signal(barrier, inc=1, device_id=gy_peer(i), device_id_type=pl.DeviceIdType.MESH)

    lane = lax.broadcasted_iota(I32, (8, 128), 1)
    sub = lax.broadcasted_iota(I32, (8, 128), 0)
    zero_row = jnp.zeros((8, 128), F32)
    for ref in (h0, hu0, hv0, z0):
        ref[ROWS] = zero_row
    m0[ROWS] = jnp.zeros((8, 128), I32)
    for ref in (h1, hu1, hv1):
        ref[ROWS + 1] = zero_row
    cpt[2] = jnp.zeros((16, 128), F32)

    slot = slots[...]
    sec = sections[...]
    coef = coefs[...]
    tile_of = slot >> 4
    k_of = slot & 15
    pipe = jnp.zeros((16, 128), F32)
    for b in range(4):
        part = lanes_at(heads[:, pl.ds(128 * b, 128)], sec & 127)
        pipe = jnp.where((sec >> 7) == b, part, pipe)
    tile_iota = lax.broadcasted_iota(I32, (128, 128), 0)
    k_iota = lax.broadcasted_iota(I32, (16, 128), 0)
    left = []
    right = []
    for l in range(16):
        left.append((jnp.broadcast_to(tile_of[l : l + 1], (128, 128)) == tile_iota).astype(F32).astype(BF16))
        hit = jnp.broadcast_to(k_of[l : l + 1], (16, 128)) == k_iota
        both = jnp.concatenate(
            [
                jnp.where(hit, jnp.broadcast_to(coef[l : l + 1], (16, 128)), 0.0),
                jnp.where(hit, jnp.broadcast_to(pipe[l : l + 1], (16, 128)), 0.0),
            ],
            axis=0,
        )
        right.append(jnp.concatenate(thirds(both), axis=0))
    by_slot = lax.dot_general(
        jnp.concatenate(right, axis=1), jnp.concatenate(left, axis=1), NT, preferred_element_type=F32
    )
    by_slot = by_slot[0:32] + by_slot[32:64] + by_slot[64:96]

    strip = strips[0].T
    strip_row = strip >> 3
    strip_j = strip & 7
    for f in (0, 1):
        for j in range(8):
            load(f, j).wait()
    lane2 = lax.broadcasted_iota(I32, (8, 256), 1)

    def level_rows(t, sums):
        for i in range(UNROLL):
            r = t * UNROLL + i
            lev = h0[r] + z0[r]
            level[r] = lev
            sums = jnp.where(lane2 == r, jnp.sum(lev, axis=1, keepdims=True), sums)
        return sums

    sums = lax.fori_loop(0, ROWS // UNROLL, level_rows, jnp.zeros((8, 256), F32))
    level[ROWS] = zero_row
    by_strip = jnp.zeros((16, 128), F32)
    for half in range(2):
        for j in range(8):
            row = jnp.broadcast_to(sums[j : j + 1, 128 * half : 128 * half + 128], (16, 128))
            part = lanes_at(row, strip_row & 127)
            by_strip = jnp.where((strip_j == j) & ((strip_row >> 7) == half), part, by_strip)
    packed = jnp.concatenate([by_slot, by_strip, jnp.zeros((80, 128), F32)], axis=0).T
    msg[...] = packed.reshape(NGX, NGY, 128)

    pl.semaphore_wait(barrier, NGX + NGY - 2)

    def phase1(i):
        return pltpu.make_async_remote_copy(
            src_ref=msg.at[lax.rem(gx + i, NGX)],
            dst_ref=mid.at[gx],
            send_sem=p1_send.at[i - 1],
            recv_sem=p1_recv.at[i - 1],
            device_id=gx_peer(i),
            device_id_type=pl.DeviceIdType.MESH,
        )

    for i in range(1, NGX):
        phase1(i).start()
    mid[gx] = msg[gx]

    for f in (2, 3, 4):
        for j in range(8):
            load(f, j).wait()

    def rows_of(r):
        return (h0[r], hu0[r], hv0[r], m0[r].astype(F32), z0[r])

    for side, r in ((0, 0), (1, ROWS - 1)):
        for f, value in enumerate(rows_of(r)):
            row_snd1[side, f] = value

    def halo_rows(snd, rcv, side, base):
        return pltpu.make_async_remote_copy(
            src_ref=snd.at[side],
            dst_ref=rcv.at[1 - side],
            send_sem=halo_send.at[base + side],
            recv_sem=halo_recv.at[base + side],
            device_id=gx_peer(NGX - 1 if side == 0 else 1),
            device_id_type=pl.DeviceIdType.MESH,
        )

    def halo_cols(snd, rcv, side, base):
        return pltpu.make_async_remote_copy(
            src_ref=snd.at[side],
            dst_ref=rcv.at[1 - side],
            send_sem=halo_send.at[base + 2 + side],
            recv_sem=halo_recv.at[base + 2 + side],
            device_id=gy_peer(NGY - 1 if side == 0 else 1),
            device_id_type=pl.DeviceIdType.MESH,
        )

    for side in (0, 1):
        halo_rows(row_snd1, row_rcv1, side, 0).start()

    lane_col = lax.broadcasted_iota(I32, (ROWS, 128), 1)

    def slab(ref, first, j):
        return ref.reshape(ref.shape[0] * 8, 128)[pl.ds(first * 8 + j, ROWS, stride=8), :]

    def pack_columns(refs, first):
        total = jnp.zeros((ROWS, 128), F32)
        for f, ref in enumerate(refs):
            low = slab(ref, first, 0).astype(F32)
            high = slab(ref, first, 7).astype(F32)
            total = jnp.where(lane_col == f, pltpu.roll(low, f, 1) if f else low, total)
            total = jnp.where(lane_col == 8 + f, pltpu.roll(high, 9 + f, 1), total)
        return total.T[0:16]

    cols1 = pack_columns((h0, hu0, hv0, m0, z0), 0)
    for side in (0, 1):
        col_snd1[side] = cols1[8 * side : 8 * side + 8]
    for side in (0, 1):
        halo_cols(col_snd1, col_rcv1, side, 0).start()

    for i in range(1, NGX):
        phase1(i).wait_recv()
    mid_flat = mid.reshape(NGX * NGY, 128)
    for b in range(NGY):
        mid_t[b] = mid_flat[pl.ds(b, NGX, stride=NGY), :]

    def phase2(i):
        return pltpu.make_async_remote_copy(
            src_ref=mid_t.at[lax.rem(gy + i, NGY)],
            dst_ref=got.at[gy],
            send_sem=p2_send.at[i - 1],
            recv_sem=p2_recv.at[i - 1],
            device_id=gy_peer(i),
            device_id_type=pl.DeviceIdType.MESH,
        )

    for i in range(1, NGY):
        phase2(i).start()
    got[gy] = mid_t[gy]

    row_iota = lax.broadcasted_iota(I32, (ROWS, 128), 0)
    for k in range(16):
        hit = jnp.broadcast_to(strip_row[k : k + 1], (ROWS, 128)) == row_iota
        onehot[:, pl.ds(128 * k, 128)] = hit.astype(F32).astype(BF16)

    last_lane = lane == 127
    first_lane = lane == 0
    corner_r = (lane == 127) & (sub == 7)
    corner_l = (lane == 0) & (sub == 0)

    def from_right(x):
        a = pltpu.roll(x, 127, 1)
        return jnp.where(last_lane, pltpu.roll(a, 7, 0), a)

    def from_left(x):
        a = pltpu.roll(x, 1, 1)
        return jnp.where(first_lane, pltpu.roll(a, 1, 0), a)

    def inner_y(q, wall):
        r = {name: from_right(q[name]) for name in ("h", "hu", "hv", "uv", "vv", "sy")}
        flux = face_y(wall, q, r)
        return tuple(f - from_left(f) for f in flux)

    NAMES = ("h", "hu", "hv", "uu", "uv", "sx")

    def step_rows(r, carry, fields, om, wx, wy, sx, sy, outs, drain):
        prev, part = carry
        q = prim(*fields, om)
        fx = face_x(wx, prev, q)
        out_h_ref, out_hu_ref, out_hv_ref = outs
        out_h_ref[r] = part[0] - fx[0]
        out_hu_ref[r] = part[1] - fx[1] - prev["h"] * sx
        out_hv_ref[r] = part[2] - fx[2]
        dy = inner_y(q, wy)
        part_h = q["h"] - dy[0] + fx[0]
        if drain is not None:
            part_h = part_h - drain
        part = (part_h, q["hu"] - dy[1] + fx[1], q["hv"] - dy[2] - q["h"] * sy + fx[2])
        return {name: q[name] for name in NAMES}, part

    no_row = ({name: zero_row for name in NAMES}, (zero_row,) * 3)

    def first_row(r, carry):
        state, m_prev, z_prev, z_prev2 = carry
        m = m0[r].astype(F32)
        z = z0[r]
        om = 1.0 - m
        wx = (HALF_DT * m_prev) * m
        wy = jnp.where(corner_r, 0.0, (HALF_DT * m) * from_right(m))
        sx = (SLOPE * m_prev) * (z - z_prev2)
        zr = jnp.where(corner_r, 0.0, from_right(z))
        zl = jnp.where(corner_l, 0.0, from_left(z))
        sy = (SLOPE * m) * (zr - zl)
        om_s[r] = om
        wx_s[r] = wx
        wy_s[r] = wy
        sx_s[r] = sx
        sy_s[r] = sy
        state = step_rows(
            r, state, (h0[r], hu0[r], hv0[r]), om, wx, wy, sx, sy, (h1, hu1, hv1), None
        )
        return state, m, z, z_prev

    def first_rows(t, carry):
        for i in range(UNROLL):
            carry = first_row(t * UNROLL + i, carry)
        return carry

    carry = lax.fori_loop(0, ROWS // UNROLL, first_rows, (no_row, zero_row, zero_row, zero_row))
    first_row(ROWS, carry)

    def edge_faces_x(rows, halo, halo_m, halo_z, mine_m):
        out = []
        for side in (0, 1):
            mine = prim(*rows[side], 1.0 - mine_m[side])
            other = prim(*halo[side], 1.0 - halo_m[side])
            wall = (HALF_DT * halo_m[side]) * mine_m[side]
            slope = (SLOPE * mine_m[side]) * (halo_z[side] * mine["h"])
            if side == 0:
                f = face_x(wall, other, mine)
                out.append((f[0], f[1] + slope, f[2]))
            else:
                f = face_x(wall, mine, other)
                out.append((-f[0], -f[1] - slope, -f[2]))
        return out

    def edge_faces_y(cols, halo, halo_m, halo_z, mine_m):
        out = []
        for side in (0, 1):
            mine = prim(*cols[side], 1.0 - mine_m[side])
            other = prim(*halo[side], 1.0 - halo_m[side])
            wall = (HALF_DT * halo_m[side]) * mine_m[side]
            slope = (SLOPE * mine_m[side]) * (halo_z[side] * mine["h"])
            if side == 0:
                f = face_y(wall, other, mine)
                out.append((f[0], f[1], f[2] + slope))
            else:
                f = face_y(wall, mine, other)
                out.append((-f[0], -f[1], -f[2] - slope))
        return out

    def add_columns(refs, first, faces):
        rows = []
        for side in (0, 1):
            rows += list(faces[side]) + [jnp.zeros((5, ROWS), F32)]
        by_row = jnp.concatenate(rows + [jnp.zeros((112, ROWS), F32)], axis=0).T
        for f, ref in enumerate(refs):
            flat = ref.reshape(ref.shape[0] * 8, 128)
            low = pl.ds(first * 8, ROWS, stride=8)
            high = pl.ds(first * 8 + 7, ROWS, stride=8)
            more = pltpu.roll(by_row, 128 - f, 1) if f else by_row
            flat[low, :] = flat[low, :] + jnp.where(lane_col == 0, more, 0.0)
            more = pltpu.roll(by_row, 127 - 8 - f, 1)
            flat[high, :] = flat[high, :] + jnp.where(lane_col == 127, more, 0.0)

    for side in (0, 1):
        halo_rows(row_snd1, row_rcv1, side, 0).wait()
        halo_cols(col_snd1, col_rcv1, side, 0).wait()
    exists_x = (gx > 0, gx < NGX - 1)
    exists_y = (gy > 0, gy < NGY - 1)

    def keep(yes, x):
        return jnp.where(yes, x, 0.0)

    halo_x = [[keep(exists_x[side], row_rcv1[side, f]) for f in range(5)] for side in (0, 1)]
    mine_x = [[row_snd1[side, f] for f in range(5)] for side in (0, 1)]
    halo_y = [[keep(exists_y[side], col_rcv1[side, f : f + 1]) for f in range(5)] for side in (0, 1)]
    mine_y = [[col_snd1[side, f : f + 1] for f in range(5)] for side in (0, 1)]
    hmx = [halo_x[s][3] for s in (0, 1)]
    hzx = [halo_x[s][4] for s in (0, 1)]
    mmx = [mine_x[s][3] for s in (0, 1)]
    hmy = [halo_y[s][3] for s in (0, 1)]
    hzy = [halo_y[s][4] for s in (0, 1)]
    mmy = [mine_y[s][3] for s in (0, 1)]
    faces = edge_faces_x([mine_x[s][:3] for s in (0, 1)], [halo_x[s][:3] for s in (0, 1)], hmx, hzx, mmx)
    for side, r in ((0, 1), (1, ROWS)):
        for f, ref in enumerate((h1, hu1, hv1)):
            ref[r] = ref[r] + faces[side][f]
    faces = edge_faces_y([mine_y[s][:3] for s in (0, 1)], [halo_y[s][:3] for s in (0, 1)], hmy, hzy, mmy)
    add_columns((h1, hu1, hv1), 1, faces)
    cols2 = pack_columns((h1, hu1, hv1), 1)

    for i in range(1, NGY):
        phase2(i).wait_recv()
    got_flat = got.reshape(NGX * NGY, 128)
    arrived = jnp.concatenate([got_flat[pl.ds(a, NGY, stride=NGX), :] for a in range(NGX)], axis=0).T
    right = []
    j_iota = lax.broadcasted_iota(I32, (8, 128), 0)
    for k in range(16):
        hit = jnp.broadcast_to(strip_j[k : k + 1], (8, 128)) == j_iota
        both = jnp.concatenate(
            [
                jnp.where(hit, jnp.broadcast_to(arrived[k : k + 1], (8, 128)), 0.0),
                jnp.where(hit, jnp.broadcast_to(arrived[16 + k : 17 + k], (8, 128)), 0.0),
            ],
            axis=0,
        )
        right.append(jnp.concatenate(thirds(both), axis=0))
    by_row = lax.dot_general(jnp.concatenate(right, axis=1), onehot[...], NT, preferred_element_type=F32)
    by_row = by_row[0:16] + by_row[16:32] + by_row[32:48]
    for half in range(2):
        cpt[half] = by_row[:, 128 * half : 128 * half + 128]

    def drain_of(r):
        half = r // 128
        at = jnp.full((8, 128), r - half * 128, I32)
        c = lanes_at(cpt[half, 0:8], at)
        p = lanes_at(cpt[half, 8:16], at)
        return (DT * c) * (level[r] - p)

    own_x = []
    for side, r in ((0, 0), (1, ROWS - 1)):
        own_x.append((h1[r + 1] - drain_of(r), hu1[r + 1], hv1[r + 1]))
        for f in range(3):
            row_snd2[side, f] = own_x[side][f]
    own_y = []
    for side, j in ((0, 0), (1, 7)):
        lev = mine_y[side][0] + mine_y[side][4]
        less = (DT * by_row[j : j + 1]) * (lev - by_row[8 + j : 9 + j])
        c = cols2[8 * side : 8 * side + 8]
        own_y.append((c[0:1] - less, c[1:2], c[2:3]))
        col_snd2[side] = jnp.concatenate(list(own_y[side]) + [jnp.zeros((5, ROWS), F32)], axis=0)
    for side in (0, 1):
        halo_rows(row_snd2, row_rcv2, side, 4).start()
        halo_cols(col_snd2, col_rcv2, side, 4).start()

    def second_row(r, state):
        less = drain_of(r)
        fields = (h1[r + 1] - less, hu1[r + 1], hv1[r + 1])
        return step_rows(
            r, state, fields, om_s[r], wx_s[r], wy_s[r], sx_s[r], sy_s[r], (h2, hu2, hv2), less
        )

    def second_rows(t, state):
        for i in range(UNROLL):
            state = second_row(t * UNROLL + i, state)
        return state

    state = lax.fori_loop(0, ROWS // UNROLL, second_rows, no_row)
    second_row(ROWS, state)

    for side in (0, 1):
        halo_rows(row_snd2, row_rcv2, side, 4).wait()
        halo_cols(col_snd2, col_rcv2, side, 4).wait()
    halo_x = [[keep(exists_x[side], row_rcv2[side, f]) for f in range(3)] for side in (0, 1)]
    halo_y = [[keep(exists_y[side], col_rcv2[side, f : f + 1]) for f in range(3)] for side in (0, 1)]
    faces = edge_faces_x(own_x, halo_x, hmx, hzx, mmx)
    for side, r in ((0, 1), (1, ROWS)):
        for f, ref in enumerate((h2, hu2, hv2)):
            ref[r] = ref[r] + faces[side][f]

    outs = ((h2, out_h), (hu2, out_hu), (hv2, out_hv))

    def store(f, j):
        src, dst = outs[f]
        return pltpu.make_async_copy(
            src.at[pl.ds(1, ROWS), j, :], dst.at[:, pl.ds(128 * j, 128)], out_sem.at[f, j]
        )

    for f in range(3):
        for j in range(1, 7):
            store(f, j).start()
    faces = edge_faces_y(own_y, halo_y, hmy, hzy, mmy)
    add_columns((h2, hu2, hv2), 1, faces)
    for f in range(3):
        for j in (0, 7):
            store(f, j).start()

    level_sum = jnp.zeros((16, 128), F32)
    for k in range(16):
        row = jnp.broadcast_to(arrived[32 + k : 33 + k], (16, 128))
        level_sum = jnp.where(k_of == k, lanes_at(row, tile_of & 127), level_sum)
    rate = jnp.where(slot >= 0, coef * (level_sum - 128.0 * pipe), 0.0)
    block = lax.broadcasted_iota(I32, (8, 128), 0)
    for l in range(16):
        s_row = sec[l : l + 1]
        hit = (jnp.broadcast_to(s_row & 127, (128, 128)) == tile_iota).astype(F32).astype(BF16)
        value = jnp.where(
            jnp.broadcast_to(s_row >> 7, (8, 128)) == block, jnp.broadcast_to(rate[l : l + 1], (8, 128)), 0.0
        )
        got_l = lax.dot_general(jnp.concatenate(thirds(value), axis=0), hit, NT, preferred_element_type=F32)
        got_l = got_l[0:8] + got_l[8:16] + got_l[16:24]
        for b in range(4):
            inflow_s[l : l + 1, pl.ds(128 * b, 128)] = got_l[b : b + 1]
    share = inflow_s[...] / AREA
    head = heads[...]
    cv = conv[...]
    sec_lane = lax.broadcasted_iota(I32, (16, 512), 1)
    face_k = jnp.where(sec_lane == 511, cv, 0.5 * (cv + pltpu.roll(cv, 511, 1)))
    for turn in range(SUBSTEPS):
        below = jnp.where(sec_lane == 511, 0.0, pltpu.roll(head, 511, 1))
        leaving = face_k * (head - below)
        entering = jnp.where(sec_lane == 0, 0.0, pltpu.roll(leaving, 1, 1))
        head = head + SEWER_DT * (entering - leaving + share)
    out_sewer[...] = head

    for i in range(1, NGX):
        phase1(i).wait_send()
    for i in range(1, NGY):
        phase2(i).wait_send()
    for f in range(3):
        for j in range(8):
            store(f, j).wait()


def body(*args):
    rows, cols = args[0].shape
    field = functools.partial(pltpu.VMEM, dtype=F32)
    any_space = pl.BlockSpec(memory_space=pl.ANY)
    vmem = pl.BlockSpec(memory_space=pltpu.VMEM)
    grid = jax.ShapeDtypeStruct((rows, cols), F32)
    sewer = jax.ShapeDtypeStruct(args[9].shape, F32)
    dma = pltpu.SemaphoreType.DMA
    return pl.pallas_call(
        kernel,
        out_shape=(grid, grid, grid, sewer),
        in_specs=[any_space] * 5 + [vmem] * 6,
        out_specs=(any_space, any_space, any_space, vmem),
        scratch_shapes=[
            pltpu.VMEM((ROWS + 1, 8, 128), F32),
            pltpu.VMEM((ROWS + 1, 8, 128), F32),
            pltpu.VMEM((ROWS + 1, 8, 128), F32),
            pltpu.VMEM((ROWS + 1, 8, 128), F32),
            pltpu.VMEM((ROWS + 1, 8, 128), I32),
            pltpu.VMEM((ROWS + 1, 8, 128), F32),
        ]
        + [pltpu.VMEM((ROWS + 2, 8, 128), F32)] * 3
        + [pltpu.VMEM((ROWS + 1, 8, 128), F32)] * 8
        + [
            pltpu.VMEM((ROWS, 2048), BF16),
            pltpu.VMEM((NGX, NGY, 128), F32),
            pltpu.VMEM((NGX, NGY, 128), F32),
            pltpu.VMEM((NGY, NGX, 128), F32),
            pltpu.VMEM((NGY, NGX, 128), F32),
            pltpu.VMEM((3, 16, 128), F32),
            pltpu.VMEM((2, 5, 8, 128), F32),
            pltpu.VMEM((2, 5, 8, 128), F32),
            pltpu.VMEM((2, 3, 8, 128), F32),
            pltpu.VMEM((2, 3, 8, 128), F32),
            pltpu.VMEM((2, 8, ROWS), F32),
            pltpu.VMEM((2, 8, ROWS), F32),
            pltpu.VMEM((2, 8, ROWS), F32),
            pltpu.VMEM((2, 8, ROWS), F32),
            pltpu.VMEM((16, 512), F32),
            dma((5, 8)),
            dma((3, 8)),
            dma((NGX - 1,)),
            dma((NGX - 1,)),
            dma((NGY - 1,)),
            dma((NGY - 1,)),
            dma((8,)),
            dma((8,)),
        ],
        compiler_params=pltpu.CompilerParams(
            collective_id=0, has_side_effects=True, vmem_limit_bytes=48 * 1024 * 1024
        ),
        name="street_flood",
    )(*args)


def solution(mesh):
    tiles = P("gx", "gy")
    lines = P(("gx", "gy"), None)
    return jax.shard_map(
        body,
        mesh=mesh,
        in_specs=(tiles,) * 5 + (P(("gx", "gy"), None, None),) + (lines,) * 5,
        out_specs=(tiles, tiles, tiles, lines),
        check_vma=False,
    )
```

profile of v0, /device:TPU:1, one launch (start us, length us, event | category | flops | bytes accessed | tf_op | source)
XLA Modules:
  0.0 47.0 jit_solution(14356094992850009291)
XLA Ops:
  0.6 0.0 copy-start.3
  0.6 0.0 copy-start.2
  0.7 0.0 copy-start.4
  0.7 0.8 %copy.15.strips = s32[1,128,16]{2,1,0:T(8,128)S(1)} copy(s32[1,128,16]{1,2,0:T(8,128)} %param.16) | data formatting | bytes 16384 | tf_op args[5]
  1.5 0.0 copy-done.3
  1.5 0.0 copy-done.2
  1.5 0.0 copy-done.4
  1.5 0.0 copy-start
  1.5 1.2 %copy-done = f32[256,1024]{1,0:T(8,128)S(1)} copy-done((f32[256,1024]{1,0:T(8,128)S(1)}, f32[256,1024]{1,0:T(8,128)}, u32[]{:S(2)}) %copy-start) | copy-done | bytes 1048600
  2.7 0.0 copy-start.1
  2.7 1.2 %copy-done.1 = f32[256,1024]{1,0:T(8,128)S(1)} copy-done((f32[256,1024]{1,0:T(8,128)S(1)}, f32[256,1024]{1,0:T(8,128)}, u32[]{:S(2)}) %copy-start.1) | copy-done | bytes 1048600
  4.0 0.0 copy-start.5
  4.0 0.7 %copy-done.5 = s32[16,128]{1,0:T(8,128)S(1)} copy-done((s32[16,128]{1,0:T(8,128)S(1)}, s32[16,128]{1,0:T(8,128)}, u32[]{:S(2)}) %copy-start.5) | copy-done | bytes 8216
  4.7 0.0 copy-start.6
  4.7 0.7 %copy-done.6 = f32[16,128]{1,0:T(8,128)S(1)} copy-done((f32[16,128]{1,0:T(8,128)S(1)}, f32[16,128]{1,0:T(8,128)}, u32[]{:S(2)}) %copy-start.6) | copy-done | bytes 8216
  5.3 38.1 %street_flood.1 = (f32[256,1024]{1,0:T(8,128)S(1)}, f32[256,1024]{1,0:T(8,128)S(1)}, f32[256,1024]{1,0:T(8,128)S(1)}, f32[16,512]{1,0:T(8,128)S(1)}) custom-call(f32[256,1024]{1,0:T(8,128)S(1)} %copy-done, f32[256,1024]{1,0:T(8,128)S(1)} %copy-done.1, f32[256,1024]{1,0:T(8,128)} %mom_y.1, f32[256,1024]{1,0:T(8,128)} %bed.1, s32[256,1024]{1,0:T(8,128)} %cells.1, ...), custom_call_target="tpu_custom_call" | custom-call | tf_op jit(solution)/shard_map/street_flood/pallas_call | solution.py:546
  43.4 1.0 %copy.20 = f32[256,1024]{1,0:T(8,128)} copy(f32[256,1024]{1,0:T(8,128)S(1)} %get-tuple-element.8) | data formatting | bytes 2097152
  44.4 1.0 %copy.21 = f32[256,1024]{1,0:T(8,128)} copy(f32[256,1024]{1,0:T(8,128)S(1)} %get-tuple-element.9) | data formatting | bytes 2097152
  45.4 1.0 %copy.22 = f32[256,1024]{1,0:T(8,128)} copy(f32[256,1024]{1,0:T(8,128)S(1)} %get-tuple-element.10) | data formatting | bytes 2097152
  46.3 0.6 %copy.23 = f32[16,512]{1,0:T(8,128)} copy(f32[16,512]{1,0:T(8,128)S(1)} %get-tuple-element.11) | data formatting | bytes 65536
Async XLA Ops:
  0.6 0.8 %copy-start.3 = (f32[16,512]{1,0:T(8,128)S(1)}, f32[16,512]{1,0:T(8,128)}, u32[]{:S(2)}) copy-start(f32[16,512]{1,0:T(8,128)} %conv.1) | copy-start | bytes 98308
  0.6 0.8 %copy-start.2 = (f32[16,512]{1,0:T(8,128)S(1)}, f32[16,512]{1,0:T(8,128)}, u32[]{:S(2)}) copy-start(f32[16,512]{1,0:T(8,128)} %heads.1) | copy-start | bytes 98308
  0.7 0.8 %copy-start.4 = (s32[16,128]{1,0:T(8,128)S(1)}, s32[16,128]{1,0:T(8,128)}, u32[]{:S(2)}) copy-start(s32[16,128]{1,0:T(8,128)} %slots.1) | copy-start | bytes 24580
  1.5 1.2 %copy-start = (f32[256,1024]{1,0:T(8,128)S(1)}, f32[256,1024]{1,0:T(8,128)}, u32[]{:S(2)}) copy-start(f32[256,1024]{1,0:T(8,128)} %depth.1) | copy-start | bytes 3145732
  2.7 1.2 %copy-start.1 = (f32[256,1024]{1,0:T(8,128)S(1)}, f32[256,1024]{1,0:T(8,128)}, u32[]{:S(2)}) copy-start(f32[256,1024]{1,0:T(8,128)} %mom_x.1) | copy-start | bytes 3145732
  4.0 0.7 %copy-start.5 = (s32[16,128]{1,0:T(8,128)S(1)}, s32[16,128]{1,0:T(8,128)}, u32[]{:S(2)}) copy-start(s32[16,128]{1,0:T(8,128)} %sections.1) | copy-start | bytes 24580
  4.7 0.7 %copy-start.6 = (f32[16,128]{1,0:T(8,128)S(1)}, f32[16,128]{1,0:T(8,128)}, u32[]{:S(2)}) copy-start(f32[16,128]{1,0:T(8,128)} %coefs.1) | copy-start | bytes 24580
where the time goes:
time: 47.3 us; the launch traced here: 47 us
  Pallas kernels  38.1 us (81%)
  local copies, waits for them, and re-layouts  8.19 us (17%)
  between operations  0.7 us (1%)
    pallas_call x1, Pallas kernels, body(): pl.pallas_call(kernel, out_shape=(grid, grid, grid, sewer), in_specs=[any...  38.1 us
    unnamed x19, local copies, waits for them, and re-layouts  8.19 us

commit v1 on v0

--- a/solution.py
+++ b/solution.py
@@ -1,4 +1,3 @@
-import functools
 import math
 
 import jax
@@ -20,7 +19,7 @@
 NGX = 8
 NGY = 16
 ROWS = 256
-UNROLL = 8
+UNROLL = 16
 F32 = jnp.float32
 BF16 = jnp.bfloat16
 I32 = jnp.int32
@@ -77,15 +76,66 @@
     )
 
 
+def faces_x(rows, halo, halo_m, halo_z, mine_m):
+    out = []
+    for side in (0, 1):
+        mine = prim(*rows[side], 1.0 - mine_m[side])
+        other = prim(*halo[side], 1.0 - halo_m[side])
+        wall = (HALF_DT * halo_m[side]) * mine_m[side]
+        slope = (SLOPE * mine_m[side]) * (halo_z[side] * mine["h"])
+        if side == 0:
+            f = face_x(wall, other, mine)
+            out.append((f[0], f[1] + slope, f[2]))
+        else:
+            f = face_x(wall, mine, other)
+            out.append((-f[0], -f[1] - slope, -f[2]))
+    return out
+
+
+def faces_y(cols, halo, halo_m, halo_z, mine_m):
+    out = []
+    for side in (0, 1):
+        mine = prim(*cols[side], 1.0 - mine_m[side])
+        other = prim(*halo[side], 1.0 - halo_m[side])
+        wall = (HALF_DT * halo_m[side]) * mine_m[side]
+        slope = (SLOPE * mine_m[side]) * (halo_z[side] * mine["h"])
+        if side == 0:
+            f = face_y(wall, other, mine)
+            out.append((f[0], f[1], f[2] + slope))
+        else:
+            f = face_y(wall, mine, other)
+            out.append((-f[0], -f[1], -f[2] - slope))
+    return out
+
+
+def slab_of(ref, first, j):
+    return ref.reshape(ref.shape[0] * 8, 128), pl.ds(first * 8 + j, ROWS, stride=8)
+
+
+def faces_by_row(faces):
+    rows = []
+    for side in (0, 1):
+        rows += list(faces[side]) + [jnp.zeros((5, ROWS), F32)]
+    return jnp.concatenate(rows + [jnp.zeros((112, ROWS), F32)], axis=0).T
+
+
+def column_sum(by_row, f, side, flat, rows):
+    at = 0 if side == 0 else 127
+    lane = lax.broadcasted_iota(I32, (ROWS, 128), 1)
+    move = (at - 8 * side - f) % 128
+    more = pltpu.roll(by_row, move, 1) if move else by_row
+    return flat[rows, :] + jnp.where(lane == at, more, 0.0)
+
+
 def kernel(
-    depth, mom_x, mom_y, bed, cells, strips, slots, sections, coefs, heads, conv,
-    out_h, out_hu, out_hv, out_sewer,
-    h0, hu0, hv0, z0, m0, level, h1, hu1, hv1, h2, hu2, hv2,
-    om_s, wx_s, wy_s, sx_s, sy_s,
+    depth, mom_x, mom_y, bed, cells, strips_in, slots_in, sections_in, coefs_in, heads_in,
+    h2, hu2, hv2, edge_out, rate_out,
+    h0, hu0, hv0, z0, m0, level, h1, hu1, hv1,
+    om_s, omr_s, wx_s, wy_s, sx_s, sy_s,
+    strips, slots, sections, coefs, heads,
     onehot, msg, mid, mid_t, got, cpt,
     row_snd1, row_rcv1, row_snd2, row_rcv2, col_snd1, col_rcv1, col_snd2, col_rcv2,
-    inflow_s,
-    in_sem, out_sem, p1_send, p1_recv, p2_send, p2_recv, halo_send, halo_recv,
+    in_sem, small_sem, p1_send, p1_recv, p2_send, p2_recv, halo_send, halo_recv,
 ):
     gx = lax.axis_index("gx")
     gy = lax.axis_index("gy")
@@ -104,6 +154,13 @@
             src.at[:, pl.ds(128 * j, 128)], dst.at[pl.ds(0, ROWS), j, :], in_sem.at[f, j]
         )
 
+    small = ((slots_in, slots), (sections_in, sections), (coefs_in, coefs), (heads_in, heads), (strips_in, strips))
+
+    def load_small(i):
+        return pltpu.make_async_copy(small[i][0], small[i][1], small_sem.at[i])
+
+    for i in range(5):
+        load_small(i).start()
     for f in range(5):
         for j in range(8):
             load(f, j).start()
@@ -117,13 +174,9 @@
     lane = lax.broadcasted_iota(I32, (8, 128), 1)
     sub = lax.broadcasted_iota(I32, (8, 128), 0)
     zero_row = jnp.zeros((8, 128), F32)
-    for ref in (h0, hu0, hv0, z0):
-        ref[ROWS] = zero_row
-    m0[ROWS] = jnp.zeros((8, 128), I32)
-    for ref in (h1, hu1, hv1):
-        ref[ROWS + 1] = zero_row
-    cpt[2] = jnp.zeros((16, 128), F32)
-
+
+    for i in range(4):
+        load_small(i).wait()
     slot = slots[...]
     sec = sections[...]
     coef = coefs[...]
@@ -153,7 +206,8 @@
     )
     by_slot = by_slot[0:32] + by_slot[32:64] + by_slot[64:96]
 
-    strip = strips[0].T
+    load_small(4).wait()
+    strip = strips[0]
     strip_row = strip >> 3
     strip_j = strip & 7
     for f in (0, 1):
@@ -162,15 +216,14 @@
     lane2 = lax.broadcasted_iota(I32, (8, 256), 1)
 
     def level_rows(t, sums):
-        for i in range(UNROLL):
-            r = t * UNROLL + i
+        for i in range(32):
+            r = t * 32 + i
             lev = h0[r] + z0[r]
             level[r] = lev
             sums = jnp.where(lane2 == r, jnp.sum(lev, axis=1, keepdims=True), sums)
         return sums
 
-    sums = lax.fori_loop(0, ROWS // UNROLL, level_rows, jnp.zeros((8, 256), F32))
-    level[ROWS] = zero_row
+    sums = lax.fori_loop(0, ROWS // 32, level_rows, jnp.zeros((8, 256), F32))
     by_strip = jnp.zeros((16, 128), F32)
     for half in range(2):
         for j in range(8):
@@ -233,7 +286,8 @@
     lane_col = lax.broadcasted_iota(I32, (ROWS, 128), 1)
 
     def slab(ref, first, j):
-        return ref.reshape(ref.shape[0] * 8, 128)[pl.ds(first * 8 + j, ROWS, stride=8), :]
+        flat, rows = slab_of(ref, first, j)
+        return flat[rows, :]
 
     def pack_columns(refs, first):
         total = jnp.zeros((ROWS, 128), F32)
@@ -250,6 +304,40 @@
     for side in (0, 1):
         halo_cols(col_snd1, col_rcv1, side, 0).start()
 
+    last_lane = lane == 127
+    first_lane = lane == 0
+    corner_r = (lane == 127) & (sub == 7)
+    corner_l = (lane == 0) & (sub == 0)
+
+    def from_right(x):
+        a = pltpu.roll(x, 127, 1)
+        return jnp.where(last_lane, pltpu.roll(a, 7, 0), a)
+
+    def from_left(x):
+        a = pltpu.roll(x, 1, 1)
+        return jnp.where(first_lane, pltpu.roll(a, 1, 0), a)
+
+    def static_rows(t, carry):
+        for i in range(UNROLL):
+            r = t * UNROLL + i
+            m_prev, z_prev, z_prev2 = carry
+            m = m0[r].astype(F32)
+            z = z0[r]
+            mr = from_right(m)
+            om_s[r] = 1.0 - m
+            omr_s[r] = 1.0 - mr
+            wx_s[r] = (HALF_DT * m_prev) * m
+            wy_s[r] = jnp.where(corner_r, 0.0, (HALF_DT * m) * mr)
+            sx_s[r] = (SLOPE * m_prev) * (z - z_prev2)
+            zr = jnp.where(corner_r, 0.0, from_right(z))
+            zl = jnp.where(corner_l, 0.0, from_left(z))
+            sy_s[r] = (SLOPE * m) * (zr - zl)
+            carry = (m, z, z_prev)
+        return carry
+
+    m_end, _, z_end = lax.fori_loop(0, ROWS // UNROLL, static_rows, (zero_row,) * 3)
+    sx_s[ROWS] = (SLOPE * m_end) * (-z_end)
+
     for i in range(1, NGX):
         phase1(i).wait_recv()
     mid_flat = mid.reshape(NGX * NGY, 128)
@@ -275,115 +363,37 @@
         hit = jnp.broadcast_to(strip_row[k : k + 1], (ROWS, 128)) == row_iota
         onehot[:, pl.ds(128 * k, 128)] = hit.astype(F32).astype(BF16)
 
-    last_lane = lane == 127
-    first_lane = lane == 0
-    corner_r = (lane == 127) & (sub == 7)
-    corner_l = (lane == 0) & (sub == 0)
-
-    def from_right(x):
-        a = pltpu.roll(x, 127, 1)
-        return jnp.where(last_lane, pltpu.roll(a, 7, 0), a)
-
-    def from_left(x):
-        a = pltpu.roll(x, 1, 1)
-        return jnp.where(first_lane, pltpu.roll(a, 1, 0), a)
-
-    def inner_y(q, wall):
-        r = {name: from_right(q[name]) for name in ("h", "hu", "hv", "uv", "vv", "sy")}
-        flux = face_y(wall, q, r)
-        return tuple(f - from_left(f) for f in flux)
-
     NAMES = ("h", "hu", "hv", "uu", "uv", "sx")
 
-    def step_rows(r, carry, fields, om, wx, wy, sx, sy, outs, drain):
-        prev, part = carry
-        q = prim(*fields, om)
-        fx = face_x(wx, prev, q)
-        out_h_ref, out_hu_ref, out_hv_ref = outs
-        out_h_ref[r] = part[0] - fx[0]
-        out_hu_ref[r] = part[1] - fx[1] - prev["h"] * sx
-        out_hv_ref[r] = part[2] - fx[2]
-        dy = inner_y(q, wy)
-        part_h = q["h"] - dy[0] + fx[0]
-        if drain is not None:
-            part_h = part_h - drain
-        part = (part_h, q["hu"] - dy[1] + fx[1], q["hv"] - dy[2] - q["h"] * sy + fx[2])
-        return {name: q[name] for name in NAMES}, part
-
-    no_row = ({name: zero_row for name in NAMES}, (zero_row,) * 3)
-
-    def first_row(r, carry):
-        state, m_prev, z_prev, z_prev2 = carry
-        m = m0[r].astype(F32)
-        z = z0[r]
-        om = 1.0 - m
-        wx = (HALF_DT * m_prev) * m
-        wy = jnp.where(corner_r, 0.0, (HALF_DT * m) * from_right(m))
-        sx = (SLOPE * m_prev) * (z - z_prev2)
-        zr = jnp.where(corner_r, 0.0, from_right(z))
-        zl = jnp.where(corner_l, 0.0, from_left(z))
-        sy = (SLOPE * m) * (zr - zl)
-        om_s[r] = om
-        wx_s[r] = wx
-        wy_s[r] = wy
-        sx_s[r] = sx
-        sy_s[r] = sy
-        state = step_rows(
-            r, state, (h0[r], hu0[r], hv0[r]), om, wx, wy, sx, sy, (h1, hu1, hv1), None
-        )
-        return state, m, z, z_prev
-
-    def first_rows(t, carry):
-        for i in range(UNROLL):
-            carry = first_row(t * UNROLL + i, carry)
-        return carry
-
-    carry = lax.fori_loop(0, ROWS // UNROLL, first_rows, (no_row, zero_row, zero_row, zero_row))
-    first_row(ROWS, carry)
-
-    def edge_faces_x(rows, halo, halo_m, halo_z, mine_m):
-        out = []
-        for side in (0, 1):
-            mine = prim(*rows[side], 1.0 - mine_m[side])
-            other = prim(*halo[side], 1.0 - halo_m[side])
-            wall = (HALF_DT * halo_m[side]) * mine_m[side]
-            slope = (SLOPE * mine_m[side]) * (halo_z[side] * mine["h"])
-            if side == 0:
-                f = face_x(wall, other, mine)
-                out.append((f[0], f[1] + slope, f[2]))
-            else:
-                f = face_x(wall, mine, other)
-                out.append((-f[0], -f[1] - slope, -f[2]))
-        return out
-
-    def edge_faces_y(cols, halo, halo_m, halo_z, mine_m):
-        out = []
-        for side in (0, 1):
-            mine = prim(*cols[side], 1.0 - mine_m[side])
-            other = prim(*halo[side], 1.0 - halo_m[side])
-            wall = (HALF_DT * halo_m[side]) * mine_m[side]
-            slope = (SLOPE * mine_m[side]) * (halo_z[side] * mine["h"])
-            if side == 0:
-                f = face_y(wall, other, mine)
-                out.append((f[0], f[1], f[2] + slope))
-            else:
-                f = face_y(wall, mine, other)
-                out.append((-f[0], -f[1], -f[2] - slope))
-        return out
-
-    def add_columns(refs, first, faces):
-        rows = []
-        for side in (0, 1):
-            rows += list(faces[side]) + [jnp.zeros((5, ROWS), F32)]
-        by_row = jnp.concatenate(rows + [jnp.zeros((112, ROWS), F32)], axis=0).T
-        for f, ref in enumerate(refs):
-            flat = ref.reshape(ref.shape[0] * 8, 128)
-            low = pl.ds(first * 8, ROWS, stride=8)
-            high = pl.ds(first * 8 + 7, ROWS, stride=8)
-            more = pltpu.roll(by_row, 128 - f, 1) if f else by_row
-            flat[low, :] = flat[low, :] + jnp.where(lane_col == 0, more, 0.0)
-            more = pltpu.roll(by_row, 127 - 8 - f, 1)
-            flat[high, :] = flat[high, :] + jnp.where(lane_col == 127, more, 0.0)
+    def sweep(src, off, outs, drain):
+        def one(r, carry):
+            prev, part = carry
+            raw = [ref[r + off] for ref in src]
+            q = prim(*raw, om_s[r])
+            right = prim(*[from_right(x) for x in raw], omr_s[r])
+            fx = face_x(wx_s[r], prev, q)
+            outs[0][r] = part[0] - fx[0]
+            outs[1][r] = part[1] - fx[1] - prev["h"] * sx_s[r]
+            outs[2][r] = part[2] - fx[2]
+            dy = [f - from_left(f) for f in face_y(wy_s[r], q, right)]
+            part_h = q["h"] - dy[0] + fx[0]
+            if drain is not None:
+                part_h = part_h - drain[r]
+            part = (part_h, q["hu"] - dy[1] + fx[1], q["hv"] - dy[2] - q["h"] * sy_s[r] + fx[2])
+            return {name: q[name] for name in NAMES}, part
+
+        def some(t, carry):
+            for i in range(UNROLL):
+                carry = one(t * UNROLL + i, carry)
+            return carry
+
+        start = ({name: zero_row for name in NAMES}, (zero_row,) * 3)
+        prev, part = lax.fori_loop(0, ROWS // UNROLL, some, start)
+        outs[0][ROWS] = part[0]
+        outs[1][ROWS] = part[1] - prev["h"] * sx_s[ROWS]
+        outs[2][ROWS] = part[2]
+
+    sweep((h0, hu0, hv0), 0, (h1, hu1, hv1), None)
 
     for side in (0, 1):
         halo_rows(row_snd1, row_rcv1, side, 0).wait()
@@ -404,12 +414,16 @@
     hmy = [halo_y[s][3] for s in (0, 1)]
     hzy = [halo_y[s][4] for s in (0, 1)]
     mmy = [mine_y[s][3] for s in (0, 1)]
-    faces = edge_faces_x([mine_x[s][:3] for s in (0, 1)], [halo_x[s][:3] for s in (0, 1)], hmx, hzx, mmx)
+    faces = faces_x([mine_x[s][:3] for s in (0, 1)], [halo_x[s][:3] for s in (0, 1)], hmx, hzx, mmx)
     for side, r in ((0, 1), (1, ROWS)):
         for f, ref in enumerate((h1, hu1, hv1)):
             ref[r] = ref[r] + faces[side][f]
-    faces = edge_faces_y([mine_y[s][:3] for s in (0, 1)], [halo_y[s][:3] for s in (0, 1)], hmy, hzy, mmy)
-    add_columns((h1, hu1, hv1), 1, faces)
+    faces = faces_y([mine_y[s][:3] for s in (0, 1)], [halo_y[s][:3] for s in (0, 1)], hmy, hzy, mmy)
+    by_row = faces_by_row(faces)
+    for f, ref in enumerate((h1, hu1, hv1)):
+        for side in (0, 1):
+            flat, rows = slab_of(ref, 1, 7 * side)
+            flat[rows, :] = column_sum(by_row, f, side, flat, rows)
     cols2 = pack_columns((h1, hu1, hv1), 1)
 
     for i in range(1, NGY):
@@ -456,53 +470,91 @@
         halo_rows(row_snd2, row_rcv2, side, 4).start()
         halo_cols(col_snd2, col_rcv2, side, 4).start()
 
-    def second_row(r, state):
-        less = drain_of(r)
-        fields = (h1[r + 1] - less, hu1[r + 1], hv1[r + 1])
-        return step_rows(
-            r, state, fields, om_s[r], wx_s[r], wy_s[r], sx_s[r], sy_s[r], (h2, hu2, hv2), less
-        )
-
-    def second_rows(t, state):
-        for i in range(UNROLL):
-            state = second_row(t * UNROLL + i, state)
-        return state
-
-    state = lax.fori_loop(0, ROWS // UNROLL, second_rows, no_row)
-    second_row(ROWS, state)
+    def drain_rows(t, carry):
+        for i in range(32):
+            r = t * 32 + i
+            less = drain_of(r)
+            level[r] = less
+            h1[r + 1] = h1[r + 1] - less
+        return carry
+
+    lax.fori_loop(0, ROWS // 32, drain_rows, 0)
+    sweep((h1, hu1, hv1), 1, (h2, hu2, hv2), level)
 
     for side in (0, 1):
         halo_rows(row_snd2, row_rcv2, side, 4).wait()
         halo_cols(col_snd2, col_rcv2, side, 4).wait()
     halo_x = [[keep(exists_x[side], row_rcv2[side, f]) for f in range(3)] for side in (0, 1)]
     halo_y = [[keep(exists_y[side], col_rcv2[side, f : f + 1]) for f in range(3)] for side in (0, 1)]
-    faces = edge_faces_x(own_x, halo_x, hmx, hzx, mmx)
+    faces = faces_x(own_x, halo_x, hmx, hzx, mmx)
     for side, r in ((0, 1), (1, ROWS)):
         for f, ref in enumerate((h2, hu2, hv2)):
             ref[r] = ref[r] + faces[side][f]
 
-    outs = ((h2, out_h), (hu2, out_hu), (hv2, out_hv))
-
-    def store(f, j):
-        src, dst = outs[f]
-        return pltpu.make_async_copy(
-            src.at[pl.ds(1, ROWS), j, :], dst.at[:, pl.ds(128 * j, 128)], out_sem.at[f, j]
-        )
-
-    for f in range(3):
-        for j in range(1, 7):
-            store(f, j).start()
-    faces = edge_faces_y(own_y, halo_y, hmy, hzy, mmy)
-    add_columns((h2, hu2, hv2), 1, faces)
-    for f in range(3):
-        for j in (0, 7):
-            store(f, j).start()
+    for side in (0, 1):
+        rows = list(own_y[side]) + [mmy[side], hzy[side], hmy[side]] + halo_y[side]
+        edge_out[side] = jnp.concatenate(rows + [jnp.zeros((7, ROWS), F32)], axis=0)
 
     level_sum = jnp.zeros((16, 128), F32)
     for k in range(16):
         row = jnp.broadcast_to(arrived[32 + k : 33 + k], (16, 128))
         level_sum = jnp.where(k_of == k, lanes_at(row, tile_of & 127), level_sum)
     rate = jnp.where(slot >= 0, coef * (level_sum - 128.0 * pipe), 0.0)
+    rate_out[...] = rate
+
+    for i in range(1, NGX):
+        phase1(i).wait_send()
+    for i in range(1, NGY):
+        phase2(i).wait_send()
+
+
+def finish(
+    h2, hu2, hv2, edge, rate_in, sections_in, heads_in, conv_in,
+    out_h, out_hu, out_hv, out_sewer,
+    slabs, sections, heads, conv, inflow_s, sewer_s,
+    out_sem, small_sem, sewer_sem,
+):
+    small = ((sections_in, sections), (heads_in, heads), (conv_in, conv))
+
+    def load_small(i):
+        return pltpu.make_async_copy(small[i][0], small[i][1], small_sem.at[i])
+
+    for i in range(3):
+        load_small(i).start()
+    outs = ((h2, out_h), (hu2, out_hu), (hv2, out_hv))
+
+    def store(f, j):
+        src, dst = outs[f]
+        if j in (0, 7):
+            part = slabs.at[f, j // 7]
+        else:
+            part = src.at[pl.ds(1, ROWS), j, :]
+        return pltpu.make_async_copy(part, dst.at[:, pl.ds(128 * j, 128)], out_sem.at[f, j])
+
+    for f in range(3):
+        for j in range(1, 7):
+            store(f, j).start()
+
+    def row(side, i):
+        return edge[side, i : i + 1]
+
+    own = [[row(s, i) for i in range(3)] for s in (0, 1)]
+    halo = [[row(s, 6 + i) for i in range(3)] for s in (0, 1)]
+    faces = faces_y(
+        own, halo, [row(s, 5) for s in (0, 1)], [row(s, 4) for s in (0, 1)], [row(s, 3) for s in (0, 1)]
+    )
+    by_row = faces_by_row(faces)
+    for f, (ref, _) in enumerate(outs):
+        for side in (0, 1):
+            flat, rows = slab_of(ref, 1, 7 * side)
+            slabs[f, side] = column_sum(by_row, f, side, flat, rows)
+            store(f, 7 * side).start()
+
+    for i in range(3):
+        load_small(i).wait()
+    rate = rate_in[...]
+    sec = sections[...]
+    tile_iota = lax.broadcasted_iota(I32, (128, 128), 0)
     block = lax.broadcasted_iota(I32, (8, 128), 0)
     for l in range(16):
         s_row = sec[l : l + 1]
@@ -524,47 +576,46 @@
         leaving = face_k * (head - below)
         entering = jnp.where(sec_lane == 0, 0.0, pltpu.roll(leaving, 1, 1))
         head = head + SEWER_DT * (entering - leaving + share)
-    out_sewer[...] = head
-
-    for i in range(1, NGX):
-        phase1(i).wait_send()
-    for i in range(1, NGY):
-        phase2(i).wait_send()
+    sewer_s[...] = head
+    last = pltpu.make_async_copy(sewer_s, out_sewer, sewer_sem)
+    last.start()
     for f in range(3):
         for j in range(8):
             store(f, j).wait()
-
+    last.wait()
 
 def body(*args):
+    args = [jnp.swapaxes(a, 1, 2) if a.ndim == 3 else a for a in args]
     rows, cols = args[0].shape
-    field = functools.partial(pltpu.VMEM, dtype=F32)
-    any_space = pl.BlockSpec(memory_space=pl.ANY)
-    vmem = pl.BlockSpec(memory_space=pltpu.VMEM)
     grid = jax.ShapeDtypeStruct((rows, cols), F32)
     sewer = jax.ShapeDtypeStruct(args[9].shape, F32)
+    args = [pltpu.with_memory_space_constraint(a, pltpu.HBM) for a in args]
+    depth, mom_x, mom_y, bed, cells, strips, slots, sections, coefs, heads, conv = args
+    hbm = pl.BlockSpec(memory_space=pltpu.HBM)
+    vmem = pl.BlockSpec(memory_space=pltpu.VMEM)
     dma = pltpu.SemaphoreType.DMA
-    return pl.pallas_call(
+    padded = pltpu.VMEM((ROWS + 1, 8, 128), F32)
+    h2, hu2, hv2, edge, rate = pl.pallas_call(
         kernel,
-        out_shape=(grid, grid, grid, sewer),
-        in_specs=[any_space] * 5 + [vmem] * 6,
-        out_specs=(any_space, any_space, any_space, vmem),
-        scratch_shapes=[
-            pltpu.VMEM((ROWS + 1, 8, 128), F32),
-            pltpu.VMEM((ROWS + 1, 8, 128), F32),
-            pltpu.VMEM((ROWS + 1, 8, 128), F32),
-            pltpu.VMEM((ROWS + 1, 8, 128), F32),
-            pltpu.VMEM((ROWS + 1, 8, 128), I32),
-            pltpu.VMEM((ROWS + 1, 8, 128), F32),
-        ]
-        + [pltpu.VMEM((ROWS + 2, 8, 128), F32)] * 3
-        + [pltpu.VMEM((ROWS + 1, 8, 128), F32)] * 8
+        out_shape=(padded,) * 3
+        + (pltpu.VMEM((2, 16, ROWS), F32), pltpu.VMEM(slots.shape, F32)),
+        in_specs=[hbm] * 10,
+        out_specs=(vmem,) * 5,
+        scratch_shapes=[pltpu.VMEM((ROWS, 8, 128), F32)] * 4
+        + [pltpu.VMEM((ROWS, 8, 128), I32), pltpu.VMEM((ROWS, 8, 128), F32)]
+        + [pltpu.VMEM((ROWS + 1, 8, 128), F32)] * 9
         + [
+            pltpu.VMEM((1, 16, 128), I32),
+            pltpu.VMEM((16, 128), I32),
+            pltpu.VMEM((16, 128), I32),
+            pltpu.VMEM((16, 128), F32),
+            pltpu.VMEM((16, 512), F32),
             pltpu.VMEM((ROWS, 2048), BF16),
             pltpu.VMEM((NGX, NGY, 128), F32),
             pltpu.VMEM((NGX, NGY, 128), F32),
             pltpu.VMEM((NGY, NGX, 128), F32),
             pltpu.VMEM((NGY, NGX, 128), F32),
-            pltpu.VMEM((3, 16, 128), F32),
+            pltpu.VMEM((2, 16, 128), F32),
             pltpu.VMEM((2, 5, 8, 128), F32),
             pltpu.VMEM((2, 5, 8, 128), F32),
             pltpu.VMEM((2, 3, 8, 128), F32),
@@ -573,9 +624,8 @@
             pltpu.VMEM((2, 8, ROWS), F32),
             pltpu.VMEM((2, 8, ROWS), F32),
             pltpu.VMEM((2, 8, ROWS), F32),
-            pltpu.VMEM((16, 512), F32),
             dma((5, 8)),
-            dma((3, 8)),
+            dma((5,)),
             dma((NGX - 1,)),
             dma((NGX - 1,)),
             dma((NGY - 1,)),
@@ -584,10 +634,29 @@
             dma((8,)),
         ],
         compiler_params=pltpu.CompilerParams(
-            collective_id=0, has_side_effects=True, vmem_limit_bytes=48 * 1024 * 1024
+            collective_id=0, has_side_effects=True, vmem_limit_bytes=40 * 1024 * 1024
         ),
         name="street_flood",
-    )(*args)
+    )(depth, mom_x, mom_y, bed, cells, strips, slots, sections, coefs, heads)
+    return pl.pallas_call(
+        finish,
+        out_shape=(grid, grid, grid, sewer),
+        in_specs=[vmem] * 5 + [hbm] * 3,
+        out_specs=(hbm,) * 4,
+        scratch_shapes=[
+            pltpu.VMEM((3, 2, ROWS, 128), F32),
+            pltpu.VMEM((16, 128), I32),
+            pltpu.VMEM((16, 512), F32),
+            pltpu.VMEM((16, 512), F32),
+            pltpu.VMEM((16, 512), F32),
+            pltpu.VMEM((16, 512), F32),
+            dma((3, 8)),
+            dma((3,)),
+            dma,
+        ],
+        compiler_params=pltpu.CompilerParams(vmem_limit_bytes=16 * 1024 * 1024),
+        name="flood_finish",
+    )(h2, hu2, hv2, edge, rate, sections, heads, conv)
 
 
 def solution(mesh):

time: 47.3 us -> 30.3 us (0.64)
  Pallas kernels: 38.1 us -> 29.4 us
  local copies, waits for them, and re-layouts: 8.19 us -> 0 us
    pallas_call x1 -> x2, Pallas kernels: 38.1 us -> 29.4 us  [the longest x1 26.2 us: body(): pl.pallas_call(kernel, out_shape=(padded,) * 3 + (pltpu.VMEM((2, 16, ROWS...]
    unnamed x19 -> x0, local copies, waits for them, and re-layouts: 8.19 us -> none
where the time goes in v1:
time: 30.3 us; the launch traced here: 30.1 us
  Pallas kernels  29.4 us (97%)
  between operations  0.64 us (2%)
    pallas_call x1, Pallas kernels, body(): pl.pallas_call(kernel, out_shape=(padded,) * 3 + (pltpu.VMEM((2, 16, ROWS...  26.2 us
    pallas_call x1, Pallas kernels, body(): pl.pallas_call(finish, out_shape=(grid, grid, grid, sewer), in_specs=[vme...  3.19 us

profile of v1, /device:TPU:1, one launch (start us, length us, event | category | flops | bytes accessed | tf_op | source)
XLA Modules:
  0.0 30.1 jit_solution(3751104312365835661)
XLA Ops:
  0.6 26.2 %street_flood.1 = (f32[257,8,128]{2,1,0:T(8,128)S(1)}, f32[257,8,128]{2,1,0:T(8,128)S(1)}, f32[257,8,128]{2,1,0:T(8,128)S(1)}, f32[2,16,256]{2,1,0:T(8,128)S(1)}, f32[16,128]{1,0:T(8,128)S(1)}) custom-call(f32[256,1024]{1,0:T(8,128)} %depth.1, f32[256,1024]{1,0:T(8,128)} %mom_x.1, f32[256,1024]{1,0:T(8,128)} %mom_y.1, f32[256,1024]{1,0:T(8,128)} %bed.1, ...), custom_call_target="tpu_custom_call" | custom-call | tf_op jit(solution)/shard_map/street_flood/pallas_call | solution.py:598
  26.9 3.2 %flood_finish.1 = (f32[256,1024]{1,0:T(8,128)}, f32[256,1024]{1,0:T(8,128)}, f32[256,1024]{1,0:T(8,128)}, f32[16,512]{1,0:T(8,128)}) custom-call(f32[257,8,128]{2,1,0:T(8,128)S(1)} %get-tuple-element.9.h2, f32[257,8,128]{2,1,0:T(8,128)S(1)} %get-tuple-element.10.hu2, f32[257,8,128]{2,1,0:T(8,128)S(1)} %get-tuple-element.11.hv2, ...), custom_call_target="tpu_custom_call" | custom-call | tf_op jit(solution)/shard_map/flood_finish/pallas_call | solution.py:641

commit v2 on v1

--- a/solution.py
+++ b/solution.py
@@ -112,19 +112,27 @@
     return ref.reshape(ref.shape[0] * 8, 128), pl.ds(first * 8 + j, ROWS, stride=8)
 
 
-def faces_by_row(faces):
-    rows = []
-    for side in (0, 1):
-        rows += list(faces[side]) + [jnp.zeros((5, ROWS), F32)]
-    return jnp.concatenate(rows + [jnp.zeros((112, ROWS), F32)], axis=0).T
-
-
-def column_sum(by_row, f, side, flat, rows):
-    at = 0 if side == 0 else 127
+def edge_matrix(left, right):
+    sub = lax.broadcasted_iota(I32, (8, ROWS), 0)
+    top = jnp.where(sub == 0, jnp.broadcast_to(left, (8, ROWS)), 0.0)
+    bottom = jnp.where(sub == 7, jnp.broadcast_to(right, (8, ROWS)), 0.0)
+    return jnp.concatenate([top, jnp.zeros((112, ROWS), F32), bottom], axis=0).T
+
+
+def edge_slabs(ref, first, terms):
     lane = lax.broadcasted_iota(I32, (ROWS, 128), 1)
-    move = (at - 8 * side - f) % 128
-    more = pltpu.roll(by_row, move, 1) if move else by_row
-    return flat[rows, :] + jnp.where(lane == at, more, 0.0)
+    flat, low = slab_of(ref, first, 0)
+    _, high = slab_of(ref, first, 7)
+    return (
+        flat[low, :] + jnp.where(lane == 0, terms, 0.0),
+        flat[high, :] + jnp.where(lane == 127, terms, 0.0),
+    )
+
+
+def edge_columns(low, high):
+    lane = lax.broadcasted_iota(I32, (ROWS, 128), 1)
+    both = jnp.where(lane < 64, low, high).T
+    return both[0:1], both[127:128]
 
 
 def kernel(
@@ -133,7 +141,7 @@
     h0, hu0, hv0, z0, m0, level, h1, hu1, hv1,
     om_s, omr_s, wx_s, wy_s, sx_s, sy_s,
     strips, slots, sections, coefs, heads,
-    onehot, msg, mid, mid_t, got, cpt,
+    onehot, msg, mid, mid_t, got, slot_coef, slot_pipe, ring,
     row_snd1, row_rcv1, row_snd2, row_rcv2, col_snd1, col_rcv1, col_snd2, col_rcv2,
     in_sem, small_sem, p1_send, p1_recv, p2_send, p2_recv, halo_send, halo_recv,
 ):
@@ -283,25 +291,15 @@
     for side in (0, 1):
         halo_rows(row_snd1, row_rcv1, side, 0).start()
 
-    lane_col = lax.broadcasted_iota(I32, (ROWS, 128), 1)
-
-    def slab(ref, first, j):
-        flat, rows = slab_of(ref, first, j)
-        return flat[rows, :]
-
-    def pack_columns(refs, first):
-        total = jnp.zeros((ROWS, 128), F32)
-        for f, ref in enumerate(refs):
-            low = slab(ref, first, 0).astype(F32)
-            high = slab(ref, first, 7).astype(F32)
-            total = jnp.where(lane_col == f, pltpu.roll(low, f, 1) if f else low, total)
-            total = jnp.where(lane_col == 8 + f, pltpu.roll(high, 9 + f, 1), total)
-        return total.T[0:16]
-
-    cols1 = pack_columns((h0, hu0, hv0, m0, z0), 0)
-    for side in (0, 1):
-        col_snd1[side] = cols1[8 * side : 8 * side + 8]
-    for side in (0, 1):
+    cols1 = ([], [])
+    for ref in (h0, hu0, hv0, m0, z0):
+        flat, low = slab_of(ref, 0, 0)
+        _, high = slab_of(ref, 0, 7)
+        ends = edge_columns(flat[low, :].astype(F32), flat[high, :].astype(F32))
+        for side in (0, 1):
+            cols1[side].append(ends[side])
+    for side in (0, 1):
+        col_snd1[side] = jnp.concatenate(cols1[side] + [jnp.zeros((3, ROWS), F32)], axis=0)
         halo_cols(col_snd1, col_rcv1, side, 0).start()
 
     last_lane = lane == 127
@@ -318,8 +316,8 @@
         return jnp.where(first_lane, pltpu.roll(a, 1, 0), a)
 
     def static_rows(t, carry):
-        for i in range(UNROLL):
-            r = t * UNROLL + i
+        for i in range(32):
+            r = t * 32 + i
             m_prev, z_prev, z_prev2 = carry
             m = m0[r].astype(F32)
             z = z0[r]
@@ -335,7 +333,7 @@
             carry = (m, z, z_prev)
         return carry
 
-    m_end, _, z_end = lax.fori_loop(0, ROWS // UNROLL, static_rows, (zero_row,) * 3)
+    m_end, _, z_end = lax.fori_loop(0, ROWS // 32, static_rows, (zero_row,) * 3)
     sx_s[ROWS] = (SLOPE * m_end) * (-z_end)
 
     for i in range(1, NGX):
@@ -365,35 +363,52 @@
 
     NAMES = ("h", "hu", "hv", "uu", "uv", "sx")
 
-    def sweep(src, off, outs, drain):
-        def one(r, carry):
+    def sweep(src, off, outs, drained):
+        def ahead(r, i):
+            h = src[0][r + off]
+            if drained:
+                less = slot_coef[r] * (level[r] - slot_pipe[r])
+                h = h - less
+                ring[3, i] = less
+                ring[4, i] = h
+            ring[0, i] = from_right(h)
+            ring[1, i] = from_right(src[1][r + off])
+            ring[2, i] = from_right(src[2][r + off])
+
+        def one(r, i, carry):
             prev, part = carry
-            raw = [ref[r + off] for ref in src]
-            q = prim(*raw, om_s[r])
-            right = prim(*[from_right(x) for x in raw], omr_s[r])
+            h = ring[4, i] if drained else src[0][r + off]
+            q = prim(h, src[1][r + off], src[2][r + off], om_s[r])
+            right = prim(ring[0, i], ring[1, i], ring[2, i], omr_s[r])
             fx = face_x(wx_s[r], prev, q)
             outs[0][r] = part[0] - fx[0]
             outs[1][r] = part[1] - fx[1] - prev["h"] * sx_s[r]
             outs[2][r] = part[2] - fx[2]
             dy = [f - from_left(f) for f in face_y(wy_s[r], q, right)]
             part_h = q["h"] - dy[0] + fx[0]
-            if drain is not None:
-                part_h = part_h - drain[r]
+            if drained:
+                part_h = part_h - ring[3, i]
             part = (part_h, q["hu"] - dy[1] + fx[1], q["hv"] - dy[2] - q["h"] * sy_s[r] + fx[2])
             return {name: q[name] for name in NAMES}, part
 
+        turns = ROWS // UNROLL
+        for i in range(UNROLL):
+            ahead(i, i)
+
         def some(t, carry):
+            following = jnp.minimum(t + 1, turns - 1) * UNROLL
             for i in range(UNROLL):
-                carry = one(t * UNROLL + i, carry)
+                carry = one(t * UNROLL + i, i, carry)
+                ahead(following + i, i)
             return carry
 
         start = ({name: zero_row for name in NAMES}, (zero_row,) * 3)
-        prev, part = lax.fori_loop(0, ROWS // UNROLL, some, start)
+        prev, part = lax.fori_loop(0, turns, some, start)
         outs[0][ROWS] = part[0]
         outs[1][ROWS] = part[1] - prev["h"] * sx_s[ROWS]
         outs[2][ROWS] = part[2]
 
-    sweep((h0, hu0, hv0), 0, (h1, hu1, hv1), None)
+    sweep((h0, hu0, hv0), 0, (h1, hu1, hv1), False)
 
     for side in (0, 1):
         halo_rows(row_snd1, row_rcv1, side, 0).wait()
@@ -419,12 +434,14 @@
         for f, ref in enumerate((h1, hu1, hv1)):
             ref[r] = ref[r] + faces[side][f]
     faces = faces_y([mine_y[s][:3] for s in (0, 1)], [halo_y[s][:3] for s in (0, 1)], hmy, hzy, mmy)
-    by_row = faces_by_row(faces)
+    cols2 = []
     for f, ref in enumerate((h1, hu1, hv1)):
-        for side in (0, 1):
-            flat, rows = slab_of(ref, 1, 7 * side)
-            flat[rows, :] = column_sum(by_row, f, side, flat, rows)
-    cols2 = pack_columns((h1, hu1, hv1), 1)
+        low, high = edge_slabs(ref, 1, edge_matrix(faces[0][f], faces[1][f]))
+        flat, rows = slab_of(ref, 1, 0)
+        flat[rows, :] = low
+        flat, rows = slab_of(ref, 1, 7)
+        flat[rows, :] = high
+        cols2.append(edge_columns(low, high))
 
     for i in range(1, NGY):
         phase2(i).wait_recv()
@@ -444,15 +461,14 @@
         right.append(jnp.concatenate(thirds(both), axis=0))
     by_row = lax.dot_general(jnp.concatenate(right, axis=1), onehot[...], NT, preferred_element_type=F32)
     by_row = by_row[0:16] + by_row[16:32] + by_row[32:48]
-    for half in range(2):
-        cpt[half] = by_row[:, 128 * half : 128 * half + 128]
+    by_row = jnp.concatenate([DT * by_row[0:8], by_row[8:16]], axis=0)
 
     def drain_of(r):
-        half = r // 128
-        at = jnp.full((8, 128), r - half * 128, I32)
-        c = lanes_at(cpt[half, 0:8], at)
-        p = lanes_at(cpt[half, 8:16], at)
-        return (DT * c) * (level[r] - p)
+        lanes = by_row[:, 0:128] if r < 128 else by_row[:, 128:256]
+        at = r % 128
+        c = jnp.broadcast_to(lanes[0:8, at : at + 1], (8, 128))
+        p = jnp.broadcast_to(lanes[8:16, at : at + 1], (8, 128))
+        return c * (level[r] - p)
 
     own_x = []
     for side, r in ((0, 0), (1, ROWS - 1)):
@@ -462,24 +478,20 @@
     own_y = []
     for side, j in ((0, 0), (1, 7)):
         lev = mine_y[side][0] + mine_y[side][4]
-        less = (DT * by_row[j : j + 1]) * (lev - by_row[8 + j : 9 + j])
-        c = cols2[8 * side : 8 * side + 8]
-        own_y.append((c[0:1] - less, c[1:2], c[2:3]))
+        less = by_row[j : j + 1] * (lev - by_row[8 + j : 9 + j])
+        own_y.append((cols2[0][side] - less, cols2[1][side], cols2[2][side]))
         col_snd2[side] = jnp.concatenate(list(own_y[side]) + [jnp.zeros((5, ROWS), F32)], axis=0)
     for side in (0, 1):
         halo_rows(row_snd2, row_rcv2, side, 4).start()
         halo_cols(col_snd2, col_rcv2, side, 4).start()
 
-    def drain_rows(t, carry):
-        for i in range(32):
-            r = t * 32 + i
-            less = drain_of(r)
-            level[r] = less
-            h1[r + 1] = h1[r + 1] - less
-        return carry
-
-    lax.fori_loop(0, ROWS // 32, drain_rows, 0)
-    sweep((h1, hu1, hv1), 1, (h2, hu2, hv2), level)
+    for ref, first in ((slot_coef, 0), (slot_pipe, 8)):
+        for half in range(2):
+            for j in range(8):
+                value = by_row[first + j : first + j + 1, 128 * half : 128 * half + 128]
+                flat = ref.reshape(ROWS * 8, 128)
+                flat[pl.ds(1024 * half + j, 128, stride=8), :] = jnp.broadcast_to(value, (128, 128)).T
+    sweep((h1, hu1, hv1), 1, (h2, hu2, hv2), True)
 
     for side in (0, 1):
         halo_rows(row_snd2, row_rcv2, side, 4).wait()
@@ -543,11 +555,10 @@
     faces = faces_y(
         own, halo, [row(s, 5) for s in (0, 1)], [row(s, 4) for s in (0, 1)], [row(s, 3) for s in (0, 1)]
     )
-    by_row = faces_by_row(faces)
     for f, (ref, _) in enumerate(outs):
+        both = edge_slabs(ref, 1, edge_matrix(faces[0][f], faces[1][f]))
         for side in (0, 1):
-            flat, rows = slab_of(ref, 1, 7 * side)
-            slabs[f, side] = column_sum(by_row, f, side, flat, rows)
+            slabs[f, side] = both[side]
             store(f, 7 * side).start()
 
     for i in range(3):
@@ -571,10 +582,11 @@
     cv = conv[...]
     sec_lane = lax.broadcasted_iota(I32, (16, 512), 1)
     face_k = jnp.where(sec_lane == 511, cv, 0.5 * (cv + pltpu.roll(cv, 511, 1)))
+    above_k = jnp.where(sec_lane == 0, 0.0, pltpu.roll(face_k, 1, 1))
     for turn in range(SUBSTEPS):
         below = jnp.where(sec_lane == 511, 0.0, pltpu.roll(head, 511, 1))
         leaving = face_k * (head - below)
-        entering = jnp.where(sec_lane == 0, 0.0, pltpu.roll(leaving, 1, 1))
+        entering = above_k * (pltpu.roll(head, 1, 1) - head)
         head = head + SEWER_DT * (entering - leaving + share)
     sewer_s[...] = head
     last = pltpu.make_async_copy(sewer_s, out_sewer, sewer_sem)
@@ -615,7 +627,9 @@
             pltpu.VMEM((NGX, NGY, 128), F32),
             pltpu.VMEM((NGY, NGX, 128), F32),
             pltpu.VMEM((NGY, NGX, 128), F32),
-            pltpu.VMEM((2, 16, 128), F32),
+            pltpu.VMEM((ROWS, 8, 128), F32),
+            pltpu.VMEM((ROWS, 8, 128), F32),
+            pltpu.VMEM((5, UNROLL, 8, 128), F32),
             pltpu.VMEM((2, 5, 8, 128), F32),
             pltpu.VMEM((2, 5, 8, 128), F32),
             pltpu.VMEM((2, 3, 8, 128), F32),

time: 30.3 us -> 27.5 us (0.908)
  Pallas kernels: 29.4 us -> 26.6 us
    pallas_call x1, Pallas kernels: 26.2 us -> 23.9 us  [body(): pl.pallas_call(kernel, out_shape=(padded,) * 3 + (pltpu.VMEM((2, 16, ROWS...]
    pallas_call x1, Pallas kernels: 3.19 us -> 2.73 us  [body(): pl.pallas_call(finish, out_shape=(grid, grid, grid, sewer), in_specs=[vme...]
where the time goes in v2:
time: 27.5 us; the launch traced here: 27.2 us
  Pallas kernels  26.6 us (97%)
  between operations  0.64 us (2%)
    pallas_call x1, Pallas kernels, body(): pl.pallas_call(kernel, out_shape=(padded,) * 3 + (pltpu.VMEM((2, 16, ROWS...  23.9 us
    pallas_call x1, Pallas kernels, body(): pl.pallas_call(finish, out_shape=(grid, grid, grid, sewer), in_specs=[vme...  2.73 us

profile of v2, /device:TPU:1, one launch (start us, length us, event | category | flops | bytes accessed | tf_op | source)
XLA Modules:
  0.0 27.2 jit_solution(2018017255974817766)
XLA Ops:
  0.6 23.9 %street_flood.1 = (f32[257,8,128]{2,1,0:T(8,128)S(1)}, f32[257,8,128]{2,1,0:T(8,128)S(1)}, f32[257,8,128]{2,1,0:T(8,128)S(1)}, f32[2,16,256]{2,1,0:T(8,128)S(1)}, f32[16,128]{1,0:T(8,128)S(1)}) custom-call(f32[256,1024]{1,0:T(8,128)} %depth.1, f32[256,1024]{1,0:T(8,128)} %mom_x.1, f32[256,1024]{1,0:T(8,128)} %mom_y.1, f32[256,1024]{1,0:T(8,128)} %bed.1, ...), custom_call_target="tpu_custom_call" | custom-call | tf_op jit(solution)/shard_map/street_flood/pallas_call | solution.py:610
  24.5 2.7 %flood_finish.1 = (f32[256,1024]{1,0:T(8,128)}, f32[256,1024]{1,0:T(8,128)}, f32[256,1024]{1,0:T(8,128)}, f32[16,512]{1,0:T(8,128)}) custom-call(f32[257,8,128]{2,1,0:T(8,128)S(1)} %get-tuple-element.9.h2, f32[257,8,128]{2,1,0:T(8,128)S(1)} %get-tuple-element.10.hu2, f32[257,8,128]{2,1,0:T(8,128)S(1)} %get-tuple-element.11.hv2, ...), custom_call_target="tpu_custom_call" | custom-call | tf_op jit(solution)/shard_map/flood_finish/pallas_call | solution.py:655

commit v3 on v2

--- a/solution.py
+++ b/solution.py
@@ -136,11 +136,11 @@
 
 
 def kernel(
-    depth, mom_x, mom_y, bed, cells, strips_in, slots_in, sections_in, coefs_in, heads_in,
-    h2, hu2, hv2, edge_out, rate_out,
+    depth, mom_x, mom_y, bed, cells, strips_in, slots_in, sections_in, coefs_in, heads_in, conv_in,
+    h2, hu2, hv2, edge_out, inflow_out, sewer_in,
     h0, hu0, hv0, z0, m0, level, h1, hu1, hv1,
     om_s, omr_s, wx_s, wy_s, sx_s, sy_s,
-    strips, slots, sections, coefs, heads,
+    strips, slots, sections, coefs, heads, conv,
     onehot, msg, mid, mid_t, got, slot_coef, slot_pipe, ring,
     row_snd1, row_rcv1, row_snd2, row_rcv2, col_snd1, col_rcv1, col_snd2, col_rcv2,
     in_sem, small_sem, p1_send, p1_recv, p2_send, p2_recv, halo_send, halo_recv,
@@ -156,20 +156,30 @@
 
     pairs = ((depth, h0), (bed, z0), (cells, m0), (mom_x, hu0), (mom_y, hv0))
 
-    def load(f, j):
+    def load(f, j, part=None):
         src, dst = pairs[f]
+        rows = pl.ds(0, ROWS) if part is None else pl.ds(part * (ROWS // 2), ROWS // 2)
         return pltpu.make_async_copy(
-            src.at[:, pl.ds(128 * j, 128)], dst.at[pl.ds(0, ROWS), j, :], in_sem.at[f, j]
-        )
-
-    small = ((slots_in, slots), (sections_in, sections), (coefs_in, coefs), (heads_in, heads), (strips_in, strips))
+            src.at[rows, pl.ds(128 * j, 128)], dst.at[rows, j, :], in_sem.at[f, part or 0]
+        )
+
+    def loaded(f, part=None):
+        rows = pl.ds(0, ROWS) if part is None else pl.ds(part * (ROWS // 2), ROWS // 2)
+        whole = pairs[f][1].at[rows]
+        return pltpu.make_async_copy(whole, whole, in_sem.at[f, part or 0])
+
+    small = ((slots_in, slots), (sections_in, sections), (coefs_in, coefs), (heads_in, heads), (strips_in, strips), (conv_in, conv))
 
     def load_small(i):
         return pltpu.make_async_copy(small[i][0], small[i][1], small_sem.at[i])
 
-    for i in range(5):
+    for i in range(6):
         load_small(i).start()
-    for f in range(5):
+    for part in (0, 1):
+        for f in (0, 1):
+            for j in range(8):
+                load(f, j, part).start()
+    for f in (2, 3, 4):
         for j in range(8):
             load(f, j).start()
 
@@ -218,9 +228,6 @@
     strip = strips[0]
     strip_row = strip >> 3
     strip_j = strip & 7
-    for f in (0, 1):
-        for j in range(8):
-            load(f, j).wait()
     lane2 = lax.broadcasted_iota(I32, (8, 256), 1)
 
     def level_rows(t, sums):
@@ -231,7 +238,11 @@
             sums = jnp.where(lane2 == r, jnp.sum(lev, axis=1, keepdims=True), sums)
         return sums
 
-    sums = lax.fori_loop(0, ROWS // 32, level_rows, jnp.zeros((8, 256), F32))
+    sums = jnp.zeros((8, 256), F32)
+    for part in (0, 1):
+        for f in (0, 1):
+            loaded(f, part).wait()
+        sums = lax.fori_loop(4 * part, 4 * part + 4, level_rows, sums)
     by_strip = jnp.zeros((16, 128), F32)
     for half in range(2):
         for j in range(8):
@@ -247,8 +258,8 @@
         return pltpu.make_async_remote_copy(
             src_ref=msg.at[lax.rem(gx + i, NGX)],
             dst_ref=mid.at[gx],
-            send_sem=p1_send.at[i - 1],
-            recv_sem=p1_recv.at[i - 1],
+            send_sem=p1_send,
+            recv_sem=p1_recv,
             device_id=gx_peer(i),
             device_id_type=pl.DeviceIdType.MESH,
         )
@@ -257,51 +268,7 @@
         phase1(i).start()
     mid[gx] = msg[gx]
 
-    for f in (2, 3, 4):
-        for j in range(8):
-            load(f, j).wait()
-
-    def rows_of(r):
-        return (h0[r], hu0[r], hv0[r], m0[r].astype(F32), z0[r])
-
-    for side, r in ((0, 0), (1, ROWS - 1)):
-        for f, value in enumerate(rows_of(r)):
-            row_snd1[side, f] = value
-
-    def halo_rows(snd, rcv, side, base):
-        return pltpu.make_async_remote_copy(
-            src_ref=snd.at[side],
-            dst_ref=rcv.at[1 - side],
-            send_sem=halo_send.at[base + side],
-            recv_sem=halo_recv.at[base + side],
-            device_id=gx_peer(NGX - 1 if side == 0 else 1),
-            device_id_type=pl.DeviceIdType.MESH,
-        )
-
-    def halo_cols(snd, rcv, side, base):
-        return pltpu.make_async_remote_copy(
-            src_ref=snd.at[side],
-            dst_ref=rcv.at[1 - side],
-            send_sem=halo_send.at[base + 2 + side],
-            recv_sem=halo_recv.at[base + 2 + side],
-            device_id=gy_peer(NGY - 1 if side == 0 else 1),
-            device_id_type=pl.DeviceIdType.MESH,
-        )
-
-    for side in (0, 1):
-        halo_rows(row_snd1, row_rcv1, side, 0).start()
-
-    cols1 = ([], [])
-    for ref in (h0, hu0, hv0, m0, z0):
-        flat, low = slab_of(ref, 0, 0)
-        _, high = slab_of(ref, 0, 7)
-        ends = edge_columns(flat[low, :].astype(F32), flat[high, :].astype(F32))
-        for side in (0, 1):
-            cols1[side].append(ends[side])
-    for side in (0, 1):
-        col_snd1[side] = jnp.concatenate(cols1[side] + [jnp.zeros((3, ROWS), F32)], axis=0)
-        halo_cols(col_snd1, col_rcv1, side, 0).start()
-
+    loaded(2).wait()
     last_lane = lane == 127
     first_lane = lane == 0
     corner_r = (lane == 127) & (sub == 7)
@@ -336,8 +303,51 @@
     m_end, _, z_end = lax.fori_loop(0, ROWS // 32, static_rows, (zero_row,) * 3)
     sx_s[ROWS] = (SLOPE * m_end) * (-z_end)
 
-    for i in range(1, NGX):
-        phase1(i).wait_recv()
+    for f in (3, 4):
+        loaded(f).wait()
+
+    def rows_of(r):
+        return (h0[r], hu0[r], hv0[r], m0[r].astype(F32), z0[r])
+
+    for side, r in ((0, 0), (1, ROWS - 1)):
+        for f, value in enumerate(rows_of(r)):
+            row_snd1[side, f] = value
+
+    def halo_rows(snd, rcv, side, base):
+        return pltpu.make_async_remote_copy(
+            src_ref=snd.at[side],
+            dst_ref=rcv.at[1 - side],
+            send_sem=halo_send.at[base + side],
+            recv_sem=halo_recv.at[base + side],
+            device_id=gx_peer(NGX - 1 if side == 0 else 1),
+            device_id_type=pl.DeviceIdType.MESH,
+        )
+
+    def halo_cols(snd, rcv, side, base):
+        return pltpu.make_async_remote_copy(
+            src_ref=snd.at[side],
+            dst_ref=rcv.at[1 - side],
+            send_sem=halo_send.at[base + 2 + side],
+            recv_sem=halo_recv.at[base + 2 + side],
+            device_id=gy_peer(NGY - 1 if side == 0 else 1),
+            device_id_type=pl.DeviceIdType.MESH,
+        )
+
+    for side in (0, 1):
+        halo_rows(row_snd1, row_rcv1, side, 0).start()
+
+    cols1 = ([], [])
+    for ref in (h0, hu0, hv0, m0, z0):
+        flat, low = slab_of(ref, 0, 0)
+        _, high = slab_of(ref, 0, 7)
+        ends = edge_columns(flat[low, :].astype(F32), flat[high, :].astype(F32))
+        for side in (0, 1):
+            cols1[side].append(ends[side])
+    for side in (0, 1):
+        col_snd1[side] = jnp.concatenate(cols1[side] + [jnp.zeros((3, ROWS), F32)], axis=0)
+        halo_cols(col_snd1, col_rcv1, side, 0).start()
+
+    pltpu.make_async_copy(mid.at[pl.ds(0, NGX - 1)], mid.at[pl.ds(0, NGX - 1)], p1_recv).wait()
     mid_flat = mid.reshape(NGX * NGY, 128)
     for b in range(NGY):
         mid_t[b] = mid_flat[pl.ds(b, NGX, stride=NGY), :]
@@ -346,8 +356,8 @@
         return pltpu.make_async_remote_copy(
             src_ref=mid_t.at[lax.rem(gy + i, NGY)],
             dst_ref=got.at[gy],
-            send_sem=p2_send.at[i - 1],
-            recv_sem=p2_recv.at[i - 1],
+            send_sem=p2_send,
+            recv_sem=p2_recv,
             device_id=gy_peer(i),
             device_id_type=pl.DeviceIdType.MESH,
         )
@@ -443,10 +453,33 @@
         flat[rows, :] = high
         cols2.append(edge_columns(low, high))
 
-    for i in range(1, NGY):
-        phase2(i).wait_recv()
+    pltpu.make_async_copy(got.at[pl.ds(0, NGY - 1)], got.at[pl.ds(0, NGY - 1)], p2_recv).wait()
     got_flat = got.reshape(NGX * NGY, 128)
     arrived = jnp.concatenate([got_flat[pl.ds(a, NGY, stride=NGX), :] for a in range(NGX)], axis=0).T
+    level_sum = jnp.zeros((16, 128), F32)
+    for k in range(16):
+        row = jnp.broadcast_to(arrived[32 + k : 33 + k], (16, 128))
+        level_sum = jnp.where(k_of == k, lanes_at(row, tile_of & 127), level_sum)
+    rate = jnp.where(slot >= 0, coef * (level_sum - 128.0 * pipe), 0.0)
+    block = lax.broadcasted_iota(I32, (8, 128), 0)
+    for l in range(16):
+        s_row = sec[l : l + 1]
+        hit = (jnp.broadcast_to(s_row & 127, (128, 128)) == tile_iota).astype(F32).astype(BF16)
+        value = jnp.where(
+            jnp.broadcast_to(s_row >> 7, (8, 128)) == block, jnp.broadcast_to(rate[l : l + 1], (8, 128)), 0.0
+        )
+        got_l = lax.dot_general(jnp.concatenate(thirds(value), axis=0), hit, NT, preferred_element_type=F32)
+        got_l = got_l[0:8] + got_l[8:16] + got_l[16:24]
+        for b in range(4):
+            inflow_out[l : l + 1, pl.ds(128 * b, 128)] = got_l[b : b + 1]
+
+    load_small(5).wait()
+    cv = conv[...]
+    sec_lane = lax.broadcasted_iota(I32, (16, 512), 1)
+    face_k = jnp.where(sec_lane == 511, cv, 0.5 * (cv + pltpu.roll(cv, 511, 1)))
+    sewer_in[0] = heads[...]
+    sewer_in[1] = face_k
+    sewer_in[2] = jnp.where(sec_lane == 0, 0.0, pltpu.roll(face_k, 1, 1))
     right = []
     j_iota = lax.broadcasted_iota(I32, (8, 128), 0)
     for k in range(16):
@@ -507,32 +540,16 @@
         rows = list(own_y[side]) + [mmy[side], hzy[side], hmy[side]] + halo_y[side]
         edge_out[side] = jnp.concatenate(rows + [jnp.zeros((7, ROWS), F32)], axis=0)
 
-    level_sum = jnp.zeros((16, 128), F32)
-    for k in range(16):
-        row = jnp.broadcast_to(arrived[32 + k : 33 + k], (16, 128))
-        level_sum = jnp.where(k_of == k, lanes_at(row, tile_of & 127), level_sum)
-    rate = jnp.where(slot >= 0, coef * (level_sum - 128.0 * pipe), 0.0)
-    rate_out[...] = rate
-
-    for i in range(1, NGX):
-        phase1(i).wait_send()
-    for i in range(1, NGY):
-        phase2(i).wait_send()
+    pltpu.make_async_copy(msg.at[pl.ds(0, NGX - 1)], msg.at[pl.ds(0, NGX - 1)], p1_send).wait()
+    pltpu.make_async_copy(mid_t.at[pl.ds(0, NGY - 1)], mid_t.at[pl.ds(0, NGY - 1)], p2_send).wait()
 
 
 def finish(
-    h2, hu2, hv2, edge, rate_in, sections_in, heads_in, conv_in,
+    h2, hu2, hv2, edge, inflow, sewer_in,
     out_h, out_hu, out_hv, out_sewer,
-    slabs, sections, heads, conv, inflow_s, sewer_s,
-    out_sem, small_sem, sewer_sem,
+    slabs, sewer,
+    out_sem, sewer_sem,
 ):
-    small = ((sections_in, sections), (heads_in, heads), (conv_in, conv))
-
-    def load_small(i):
-        return pltpu.make_async_copy(small[i][0], small[i][1], small_sem.at[i])
-
-    for i in range(3):
-        load_small(i).start()
     outs = ((h2, out_h), (hu2, out_hu), (hv2, out_hv))
 
     def store(f, j):
@@ -541,7 +558,7 @@
             part = slabs.at[f, j // 7]
         else:
             part = src.at[pl.ds(1, ROWS), j, :]
-        return pltpu.make_async_copy(part, dst.at[:, pl.ds(128 * j, 128)], out_sem.at[f, j])
+        return pltpu.make_async_copy(part, dst.at[:, pl.ds(128 * j, 128)], out_sem.at[f])
 
     for f in range(3):
         for j in range(1, 7):
@@ -559,42 +576,25 @@
         both = edge_slabs(ref, 1, edge_matrix(faces[0][f], faces[1][f]))
         for side in (0, 1):
             slabs[f, side] = both[side]
-            store(f, 7 * side).start()
-
-    for i in range(3):
-        load_small(i).wait()
-    rate = rate_in[...]
-    sec = sections[...]
-    tile_iota = lax.broadcasted_iota(I32, (128, 128), 0)
-    block = lax.broadcasted_iota(I32, (8, 128), 0)
-    for l in range(16):
-        s_row = sec[l : l + 1]
-        hit = (jnp.broadcast_to(s_row & 127, (128, 128)) == tile_iota).astype(F32).astype(BF16)
-        value = jnp.where(
-            jnp.broadcast_to(s_row >> 7, (8, 128)) == block, jnp.broadcast_to(rate[l : l + 1], (8, 128)), 0.0
-        )
-        got_l = lax.dot_general(jnp.concatenate(thirds(value), axis=0), hit, NT, preferred_element_type=F32)
-        got_l = got_l[0:8] + got_l[8:16] + got_l[16:24]
-        for b in range(4):
-            inflow_s[l : l + 1, pl.ds(128 * b, 128)] = got_l[b : b + 1]
-    share = inflow_s[...] / AREA
-    head = heads[...]
-    cv = conv[...]
+
+    share = inflow[...] / AREA
+    head, face_k, above_k = sewer_in[0], sewer_in[1], sewer_in[2]
     sec_lane = lax.broadcasted_iota(I32, (16, 512), 1)
-    face_k = jnp.where(sec_lane == 511, cv, 0.5 * (cv + pltpu.roll(cv, 511, 1)))
-    above_k = jnp.where(sec_lane == 0, 0.0, pltpu.roll(face_k, 1, 1))
     for turn in range(SUBSTEPS):
         below = jnp.where(sec_lane == 511, 0.0, pltpu.roll(head, 511, 1))
         leaving = face_k * (head - below)
         entering = above_k * (pltpu.roll(head, 1, 1) - head)
         head = head + SEWER_DT * (entering - leaving + share)
-    sewer_s[...] = head
-    last = pltpu.make_async_copy(sewer_s, out_sewer, sewer_sem)
-    last.start()
+    sewer[...] = head
     for f in range(3):
-        for j in range(8):
-            store(f, j).wait()
-    last.wait()
+        for side in (0, 1):
+            store(f, 7 * side).start()
+    sewer_copy = pltpu.make_async_copy(sewer, out_sewer, sewer_sem)
+    sewer_copy.start()
+    for f, (src, _) in enumerate(outs):
+        whole = src.at[pl.ds(1, ROWS)]
+        pltpu.make_async_copy(whole, whole, out_sem.at[f]).wait()
+    sewer_copy.wait()
 
 def body(*args):
     args = [jnp.swapaxes(a, 1, 2) if a.ndim == 3 else a for a in args]
@@ -607,12 +607,12 @@
     vmem = pl.BlockSpec(memory_space=pltpu.VMEM)
     dma = pltpu.SemaphoreType.DMA
     padded = pltpu.VMEM((ROWS + 1, 8, 128), F32)
-    h2, hu2, hv2, edge, rate = pl.pallas_call(
+    h2, hu2, hv2, edge, inflow, sewer_in = pl.pallas_call(
         kernel,
         out_shape=(padded,) * 3
-        + (pltpu.VMEM((2, 16, ROWS), F32), pltpu.VMEM(slots.shape, F32)),
-        in_specs=[hbm] * 10,
-        out_specs=(vmem,) * 5,
+        + (pltpu.VMEM((2, 16, ROWS), F32), pltpu.VMEM((16, 512), F32), pltpu.VMEM((3, 16, 512), F32)),
+        in_specs=[hbm] * 11,
+        out_specs=(vmem,) * 6,
         scratch_shapes=[pltpu.VMEM((ROWS, 8, 128), F32)] * 4
         + [pltpu.VMEM((ROWS, 8, 128), I32), pltpu.VMEM((ROWS, 8, 128), F32)]
         + [pltpu.VMEM((ROWS + 1, 8, 128), F32)] * 9
@@ -621,6 +621,7 @@
             pltpu.VMEM((16, 128), I32),
             pltpu.VMEM((16, 128), I32),
             pltpu.VMEM((16, 128), F32),
+            pltpu.VMEM((16, 512), F32),
             pltpu.VMEM((16, 512), F32),
             pltpu.VMEM((ROWS, 2048), BF16),
             pltpu.VMEM((NGX, NGY, 128), F32),
@@ -638,12 +639,12 @@
             pltpu.VMEM((2, 8, ROWS), F32),
             pltpu.VMEM((2, 8, ROWS), F32),
             pltpu.VMEM((2, 8, ROWS), F32),
-            dma((5, 8)),
-            dma((5,)),
-            dma((NGX - 1,)),
-            dma((NGX - 1,)),
-            dma((NGY - 1,)),
-            dma((NGY - 1,)),
+            dma((5, 2)),
+            dma((6,)),
+            dma,
+            dma,
+            dma,
+            dma,
             dma((8,)),
             dma((8,)),
         ],
@@ -651,26 +652,21 @@
             collective_id=0, has_side_effects=True, vmem_limit_bytes=40 * 1024 * 1024
         ),
         name="street_flood",
-    )(depth, mom_x, mom_y, bed, cells, strips, slots, sections, coefs, heads)
+    )(depth, mom_x, mom_y, bed, cells, strips, slots, sections, coefs, heads, conv)
     return pl.pallas_call(
         finish,
         out_shape=(grid, grid, grid, sewer),
-        in_specs=[vmem] * 5 + [hbm] * 3,
+        in_specs=[vmem] * 6,
         out_specs=(hbm,) * 4,
         scratch_shapes=[
             pltpu.VMEM((3, 2, ROWS, 128), F32),
-            pltpu.VMEM((16, 128), I32),
             pltpu.VMEM((16, 512), F32),
-            pltpu.VMEM((16, 512), F32),
-            pltpu.VMEM((16, 512), F32),
-            pltpu.VMEM((16, 512), F32),
-            dma((3, 8)),
             dma((3,)),
             dma,
         ],
         compiler_params=pltpu.CompilerParams(vmem_limit_bytes=16 * 1024 * 1024),
         name="flood_finish",
-    )(h2, hu2, hv2, edge, rate, sections, heads, conv)
+    )(h2, hu2, hv2, edge, inflow, sewer_in)
 
 
 def solution(mesh):

time: 27.5 us -> 26.4 us (0.960)
  Pallas kernels: 26.6 us -> 25.6 us
    pallas_call x1, Pallas kernels: 2.73 us -> 1.77 us  [body(): pl.pallas_call(finish, out_shape=(grid, grid, grid, sewer), in_specs=[vme...]
where the time goes in v3:
time: 26.4 us; the launch traced here: 26.3 us
  Pallas kernels  25.6 us (97%)
  between operations  0.64 us (2%)
    pallas_call x1, Pallas kernels, body(): pl.pallas_call(kernel, out_shape=(padded,) * 3 + (pltpu.VMEM((2, 16, ROWS...  23.9 us
    pallas_call x1, Pallas kernels, body(): pl.pallas_call(finish, out_shape=(grid, grid, grid, sewer), in_specs=[vme...  1.77 us

profile of v3, /device:TPU:1, one launch (start us, length us, event | category | flops | bytes accessed | tf_op | source)
XLA Modules:
  0.0 26.3 jit_solution(9132658341500841684)
XLA Ops:
  0.6 23.9 %street_flood.1 = (f32[257,8,128]{2,1,0:T(8,128)S(1)}, f32[257,8,128]{2,1,0:T(8,128)S(1)}, f32[257,8,128]{2,1,0:T(8,128)S(1)}, f32[2,16,256]{2,1,0:T(8,128)S(1)}...) custom-call(f32[256,1024]{1,0:T(8,128)} %depth.1, f32[256,1024]{1,0:T(8,128)} %mom_x.1, f32[256,1024]{1,0:T(8,128)} %mom_y.1, ...), custom_call_target="tpu_custom_call" | custom-call | tf_op jit(solution)/shard_map/street_flood/pallas_call | solution.py:610
  24.5 1.8 %flood_finish.1 = (f32[256,1024]{1,0:T(8,128)}, f32[256,1024]{1,0:T(8,128)}, f32[256,1024]{1,0:T(8,128)}, f32[16,512]{1,0:T(8,128)}) custom-call(f32[257,8,128]{2,1,0:T(8,128)S(1)} %get-tuple-element.10.h2, f32[257,8,128]{2,1,0:T(8,128)S(1)} %get-tuple-element.11.hu2, f32[257,8,128]{2,1,0:T(8,128)S(1)} %get-tuple-element.12.hv2, ...), custom_call_target="tpu_custom_call" | custom-call | tf_op jit(solution)/shard_map/flood_finish/pallas_call | solution.py:656

commit v4 on v3

--- a/solution.py
+++ b/solution.py
@@ -17,6 +17,8 @@
 HALF_G = 0.5 * GRAVITY
 SLOPE = 0.5 * GRAVITY * DT
 NGX = 8
+FAR_GY = (10, 9, 11, 6, 14, 8, 2, 5, 7, 13, 15, 1, 3, 4, 12)
+FAR_GX = (4, 3, 5, 2, 6, 1, 7)
 NGY = 16
 ROWS = 256
 UNROLL = 16
@@ -154,6 +156,12 @@
     def gy_peer(i):
         return {"gy": lax.rem(gy + i, NGY)}
 
+    barrier = pltpu.get_barrier_semaphore()
+    for i in FAR_GX:
+        pl.semaphore_signal(barrier, inc=1, device_id=gx_peer(i), device_id_type=pl.DeviceIdType.MESH)
+    for i in FAR_GY:
+        pl.semaphore_signal(barrier, inc=1, device_id=gy_peer(i), device_id_type=pl.DeviceIdType.MESH)
+
     pairs = ((depth, h0), (bed, z0), (cells, m0), (mom_x, hu0), (mom_y, hv0))
 
     def load(f, j, part=None):
@@ -182,12 +190,6 @@
     for f in (2, 3, 4):
         for j in range(8):
             load(f, j).start()
-
-    barrier = pltpu.get_barrier_semaphore()
-    for i in range(1, NGX):
-        pl.semaphore_signal(barrier, inc=1, device_id=gx_peer(i), device_id_type=pl.DeviceIdType.MESH)
-    for i in range(1, NGY):
-        pl.semaphore_signal(barrier, inc=1, device_id=gy_peer(i), device_id_type=pl.DeviceIdType.MESH)
 
     lane = lax.broadcasted_iota(I32, (8, 128), 1)
     sub = lax.broadcasted_iota(I32, (8, 128), 0)
@@ -264,7 +266,7 @@
             device_id_type=pl.DeviceIdType.MESH,
         )
 
-    for i in range(1, NGX):
+    for i in FAR_GX:
         phase1(i).start()
     mid[gx] = msg[gx]
 
@@ -347,10 +349,12 @@
         col_snd1[side] = jnp.concatenate(cols1[side] + [jnp.zeros((3, ROWS), F32)], axis=0)
         halo_cols(col_snd1, col_rcv1, side, 0).start()
 
-    pltpu.make_async_copy(mid.at[pl.ds(0, NGX - 1)], mid.at[pl.ds(0, NGX - 1)], p1_recv).wait()
-    mid_flat = mid.reshape(NGX * NGY, 128)
-    for b in range(NGY):
-        mid_t[b] = mid_flat[pl.ds(b, NGX, stride=NGY), :]
+    row_iota = lax.broadcasted_iota(I32, (ROWS, 128), 0)
+    for k in range(16):
+        hit = jnp.broadcast_to(strip_row[k : k + 1], (ROWS, 128)) == row_iota
+        onehot[:, pl.ds(128 * k, 128)] = hit.astype(F32).astype(BF16)
+
+    NAMES = ("h", "hu", "hv", "uu", "uv", "sx")
 
     def phase2(i):
         return pltpu.make_async_remote_copy(
@@ -362,18 +366,16 @@
             device_id_type=pl.DeviceIdType.MESH,
         )
 
-    for i in range(1, NGY):
-        phase2(i).start()
-    got[gy] = mid_t[gy]
-
-    row_iota = lax.broadcasted_iota(I32, (ROWS, 128), 0)
-    for k in range(16):
-        hit = jnp.broadcast_to(strip_row[k : k + 1], (ROWS, 128)) == row_iota
-        onehot[:, pl.ds(128 * k, 128)] = hit.astype(F32).astype(BF16)
-
-    NAMES = ("h", "hu", "hv", "uu", "uv", "sx")
-
-    def sweep(src, off, outs, drained):
+    def forward():
+        pltpu.make_async_copy(mid.at[pl.ds(0, NGX - 1)], mid.at[pl.ds(0, NGX - 1)], p1_recv).wait()
+        mid_flat = mid.reshape(NGX * NGY, 128)
+        for b in range(NGY):
+            mid_t[b] = mid_flat[pl.ds(b, NGX, stride=NGY), :]
+        for i in FAR_GY:
+            phase2(i).start()
+        got[gy] = mid_t[gy]
+
+    def sweep(src, off, outs, drained, pause, between):
         def ahead(r, i):
             h = src[0][r + off]
             if drained:
@@ -413,12 +415,14 @@
             return carry
 
         start = ({name: zero_row for name in NAMES}, (zero_row,) * 3)
-        prev, part = lax.fori_loop(0, turns, some, start)
+        carry = lax.fori_loop(0, pause, some, start) if pause else start
+        between()
+        prev, part = lax.fori_loop(pause, turns, some, carry)
         outs[0][ROWS] = part[0]
         outs[1][ROWS] = part[1] - prev["h"] * sx_s[ROWS]
         outs[2][ROWS] = part[2]
 
-    sweep((h0, hu0, hv0), 0, (h1, hu1, hv1), False)
+    sweep((h0, hu0, hv0), 0, (h1, hu1, hv1), False, 6, forward)
 
     for side in (0, 1):
         halo_rows(row_snd1, row_rcv1, side, 0).wait()
@@ -524,7 +528,7 @@
                 value = by_row[first + j : first + j + 1, 128 * half : 128 * half + 128]
                 flat = ref.reshape(ROWS * 8, 128)
                 flat[pl.ds(1024 * half + j, 128, stride=8), :] = jnp.broadcast_to(value, (128, 128)).T
-    sweep((h1, hu1, hv1), 1, (h2, hu2, hv2), True)
+    sweep((h1, hu1, hv1), 1, (h2, hu2, hv2), True, 0, lambda: None)
 
     for side in (0, 1):
         halo_rows(row_snd2, row_rcv2, side, 4).wait()

time: 26.4 us -> 24.7 us (0.936)
  Pallas kernels: 25.6 us -> 23.7 us
    pallas_call x1, Pallas kernels: 23.9 us -> 22 us  [body(): pl.pallas_call(kernel, out_shape=(padded,) * 3 + (pltpu.VMEM((2, 16, ROWS...]
where the time goes in v4:
time: 24.7 us; the launch traced here: 24.4 us
  Pallas kernels  23.7 us (96%)
  between operations  0.64 us (3%)
    pallas_call x1, Pallas kernels, body(): pl.pallas_call(kernel, out_shape=(padded,) * 3 + (pltpu.VMEM((2, 16, ROWS...  22 us
    pallas_call x1, Pallas kernels, body(): pl.pallas_call(finish, out_shape=(grid, grid, grid, sewer), in_specs=[vme...  1.77 us

profile of v4, /device:TPU:1, one launch (start us, length us, event | category | flops | bytes accessed | tf_op | source)
XLA Modules:
  0.0 24.4 jit_solution(1313386767132917230)
XLA Ops:
  0.6 22.0 %street_flood.1 = (f32[257,8,128]{2,1,0:T(8,128)S(1)}, f32[257,8,128]{2,1,0:T(8,128)S(1)}, f32[257,8,128]{2,1,0:T(8,128)S(1)}, f32[2,16,256]{2,1,0:T(8,128)S(1)}...) custom-call(f32[256,1024]{1,0:T(8,128)} %depth.1, f32[256,1024]{1,0:T(8,128)} %mom_x.1, f32[256,1024]{1,0:T(8,128)} %mom_y.1, ...), custom_call_target="tpu_custom_call" | custom-call | tf_op jit(solution)/shard_map/street_flood/pallas_call | solution.py:614
  22.6 1.8 %flood_finish.1 = (f32[256,1024]{1,0:T(8,128)}, f32[256,1024]{1,0:T(8,128)}, f32[256,1024]{1,0:T(8,128)}, f32[16,512]{1,0:T(8,128)}) custom-call(f32[257,8,128]{2,1,0:T(8,128)S(1)} %get-tuple-element.10.h2, f32[257,8,128]{2,1,0:T(8,128)S(1)} %get-tuple-element.11.hu2, f32[257,8,128]{2,1,0:T(8,128)S(1)} %get-tuple-element.12.hv2, ...), custom_call_target="tpu_custom_call" | custom-call | tf_op jit(solution)/shard_map/flood_finish/pallas_call | solution.py:660

commit v5 on v4

--- a/solution.py
+++ b/solution.py
@@ -143,7 +143,7 @@
     h0, hu0, hv0, z0, m0, level, h1, hu1, hv1,
     om_s, omr_s, wx_s, wy_s, sx_s, sy_s,
     strips, slots, sections, coefs, heads, conv,
-    onehot, msg, mid, mid_t, got, slot_coef, slot_pipe, ring,
+    onehot, msg, mid, mid_t, got, slot_coef, slot_pipe, hur, hvr, in_section, ring,
     row_snd1, row_rcv1, row_snd2, row_rcv2, col_snd1, col_rcv1, col_snd2, col_rcv2,
     in_sem, small_sem, p1_send, p1_recv, p2_send, p2_recv, halo_send, halo_recv,
 ):
@@ -375,7 +375,8 @@
             phase2(i).start()
         got[gy] = mid_t[gy]
 
-    def sweep(src, off, outs, drained, pause, between):
+    def sweep(src, off, outs, rolled, pause, between):
+        drained = rolled is not None
         def ahead(r, i):
             h = src[0][r + off]
             if drained:
@@ -384,14 +385,18 @@
                 ring[3, i] = less
                 ring[4, i] = h
             ring[0, i] = from_right(h)
-            ring[1, i] = from_right(src[1][r + off])
-            ring[2, i] = from_right(src[2][r + off])
+            if not drained:
+                ring[1, i] = from_right(src[1][r + off])
+                ring[2, i] = from_right(src[2][r + off])
 
         def one(r, i, carry):
             prev, part = carry
             h = ring[4, i] if drained else src[0][r + off]
             q = prim(h, src[1][r + off], src[2][r + off], om_s[r])
-            right = prim(ring[0, i], ring[1, i], ring[2, i], omr_s[r])
+            if drained:
+                right = prim(ring[0, i], rolled[0][r], rolled[1][r], omr_s[r])
+            else:
+                right = prim(ring[0, i], ring[1, i], ring[2, i], omr_s[r])
             fx = face_x(wx_s[r], prev, q)
             outs[0][r] = part[0] - fx[0]
             outs[1][r] = part[1] - fx[1] - prev["h"] * sx_s[r]
@@ -422,7 +427,7 @@
         outs[1][ROWS] = part[1] - prev["h"] * sx_s[ROWS]
         outs[2][ROWS] = part[2]
 
-    sweep((h0, hu0, hv0), 0, (h1, hu1, hv1), False, 6, forward)
+    sweep((h0, hu0, hv0), 0, (h1, hu1, hv1), None, 6, forward)
 
     for side in (0, 1):
         halo_rows(row_snd1, row_rcv1, side, 0).wait()
@@ -457,25 +462,14 @@
         flat[rows, :] = high
         cols2.append(edge_columns(low, high))
 
-    pltpu.make_async_copy(got.at[pl.ds(0, NGY - 1)], got.at[pl.ds(0, NGY - 1)], p2_recv).wait()
-    got_flat = got.reshape(NGX * NGY, 128)
-    arrived = jnp.concatenate([got_flat[pl.ds(a, NGY, stride=NGX), :] for a in range(NGX)], axis=0).T
-    level_sum = jnp.zeros((16, 128), F32)
-    for k in range(16):
-        row = jnp.broadcast_to(arrived[32 + k : 33 + k], (16, 128))
-        level_sum = jnp.where(k_of == k, lanes_at(row, tile_of & 127), level_sum)
-    rate = jnp.where(slot >= 0, coef * (level_sum - 128.0 * pipe), 0.0)
-    block = lax.broadcasted_iota(I32, (8, 128), 0)
-    for l in range(16):
-        s_row = sec[l : l + 1]
-        hit = (jnp.broadcast_to(s_row & 127, (128, 128)) == tile_iota).astype(F32).astype(BF16)
-        value = jnp.where(
-            jnp.broadcast_to(s_row >> 7, (8, 128)) == block, jnp.broadcast_to(rate[l : l + 1], (8, 128)), 0.0
-        )
-        got_l = lax.dot_general(jnp.concatenate(thirds(value), axis=0), hit, NT, preferred_element_type=F32)
-        got_l = got_l[0:8] + got_l[8:16] + got_l[16:24]
-        for b in range(4):
-            inflow_out[l : l + 1, pl.ds(128 * b, 128)] = got_l[b : b + 1]
+    def rolled_rows(t, carry):
+        for i in range(32):
+            r = t * 32 + i
+            hur[r] = from_right(hu1[r + 1])
+            hvr[r] = from_right(hv1[r + 1])
+        return carry
+
+    lax.fori_loop(0, ROWS // 32, rolled_rows, 0)
 
     load_small(5).wait()
     cv = conv[...]
@@ -484,6 +478,13 @@
     sewer_in[0] = heads[...]
     sewer_in[1] = face_k
     sewer_in[2] = jnp.where(sec_lane == 0, 0.0, pltpu.roll(face_k, 1, 1))
+    for l in range(16):
+        hit = jnp.broadcast_to(sec[l : l + 1] & 127, (128, 128)) == tile_iota
+        in_section[l] = hit.astype(F32).astype(BF16)
+
+    pltpu.make_async_copy(got.at[pl.ds(0, NGY - 1)], got.at[pl.ds(0, NGY - 1)], p2_recv).wait()
+    got_flat = got.reshape(NGX * NGY, 128)
+    arrived = jnp.concatenate([got_flat[pl.ds(a, NGY, stride=NGX), :] for a in range(NGX)], axis=0).T
     right = []
     j_iota = lax.broadcasted_iota(I32, (8, 128), 0)
     for k in range(16):
@@ -522,13 +523,29 @@
         halo_rows(row_snd2, row_rcv2, side, 4).start()
         halo_cols(col_snd2, col_rcv2, side, 4).start()
 
+    level_sum = jnp.zeros((16, 128), F32)
+    for k in range(16):
+        row = jnp.broadcast_to(arrived[32 + k : 33 + k], (16, 128))
+        level_sum = jnp.where(k_of == k, lanes_at(row, tile_of & 127), level_sum)
+    rate = jnp.where(slot >= 0, coef * (level_sum - 128.0 * pipe), 0.0)
+    block = lax.broadcasted_iota(I32, (8, 128), 0)
+    for l in range(16):
+        s_row = sec[l : l + 1]
+        value = jnp.where(
+            jnp.broadcast_to(s_row >> 7, (8, 128)) == block, jnp.broadcast_to(rate[l : l + 1], (8, 128)), 0.0
+        )
+        got_l = lax.dot_general(jnp.concatenate(thirds(value), axis=0), in_section[l], NT, preferred_element_type=F32)
+        got_l = got_l[0:8] + got_l[8:16] + got_l[16:24]
+        for b in range(4):
+            inflow_out[l : l + 1, pl.ds(128 * b, 128)] = got_l[b : b + 1]
+
     for ref, first in ((slot_coef, 0), (slot_pipe, 8)):
         for half in range(2):
             for j in range(8):
                 value = by_row[first + j : first + j + 1, 128 * half : 128 * half + 128]
                 flat = ref.reshape(ROWS * 8, 128)
                 flat[pl.ds(1024 * half + j, 128, stride=8), :] = jnp.broadcast_to(value, (128, 128)).T
-    sweep((h1, hu1, hv1), 1, (h2, hu2, hv2), True, 0, lambda: None)
+    sweep((h1, hu1, hv1), 1, (h2, hu2, hv2), (hur, hvr), 0, lambda: None)
 
     for side in (0, 1):
         halo_rows(row_snd2, row_rcv2, side, 4).wait()
@@ -634,6 +651,9 @@
             pltpu.VMEM((NGY, NGX, 128), F32),
             pltpu.VMEM((ROWS, 8, 128), F32),
             pltpu.VMEM((ROWS, 8, 128), F32),
+            pltpu.VMEM((ROWS, 8, 128), F32),
+            pltpu.VMEM((ROWS, 8, 128), F32),
+            pltpu.VMEM((16, 128, 128), BF16),
             pltpu.VMEM((5, UNROLL, 8, 128), F32),
             pltpu.VMEM((2, 5, 8, 128), F32),
             pltpu.VMEM((2, 5, 8, 128), F32),

time: 24.7 us -> 24.4 us (0.988)
  no operation moved by 1% of the time
where the time goes in v5:
time: 24.4 us; the launch traced here: 24.3 us
  Pallas kernels  23.7 us (97%)
  between operations  0.64 us (3%)
    pallas_call x1, Pallas kernels, body(): pl.pallas_call(kernel, out_shape=(padded,) * 3 + (pltpu.VMEM((2, 16, ROWS...  21.9 us
    pallas_call x1, Pallas kernels, body(): pl.pallas_call(finish, out_shape=(grid, grid, grid, sewer), in_specs=[vme...  1.77 us

profile of v5, /device:TPU:1, one launch (start us, length us, event | category | flops | bytes accessed | tf_op | source)
XLA Modules:
  0.0 24.3 jit_solution(1346474154909479783)
XLA Ops:
  0.6 21.9 %street_flood.1 = (f32[257,8,128]{2,1,0:T(8,128)S(1)}, f32[257,8,128]{2,1,0:T(8,128)S(1)}, f32[257,8,128]{2,1,0:T(8,128)S(1)}, f32[2,16,256]{2,1,0:T(8,128)S(1)}...) custom-call(f32[256,1024]{1,0:T(8,128)} %depth.1, f32[256,1024]{1,0:T(8,128)} %mom_x.1, f32[256,1024]{1,0:T(8,128)} %mom_y.1, ...), custom_call_target="tpu_custom_call" | custom-call | tf_op jit(solution)/shard_map/street_flood/pallas_call | solution.py:631
  22.5 1.8 %flood_finish.1 = (f32[256,1024]{1,0:T(8,128)}, f32[256,1024]{1,0:T(8,128)}, f32[256,1024]{1,0:T(8,128)}, f32[16,512]{1,0:T(8,128)}) custom-call(f32[257,8,128]{2,1,0:T(8,128)S(1)} %get-tuple-element.10.h2, f32[257,8,128]{2,1,0:T(8,128)S(1)} %get-tuple-element.11.hu2, f32[257,8,128]{2,1,0:T(8,128)S(1)} %get-tuple-element.12.hv2, ...), custom_call_target="tpu_custom_call" | custom-call | tf_op jit(solution)/shard_map/flood_finish/pallas_call | solution.py:680

commit v6 on v5

--- a/solution.py
+++ b/solution.py
@@ -161,6 +161,20 @@
         pl.semaphore_signal(barrier, inc=1, device_id=gx_peer(i), device_id_type=pl.DeviceIdType.MESH)
     for i in FAR_GY:
         pl.semaphore_signal(barrier, inc=1, device_id=gy_peer(i), device_id_type=pl.DeviceIdType.MESH)
+
+    def start_halo(copy, side, at, last):
+        @pl.when(at > 0 if side == 0 else at < last)
+        def _():
+            copy.start()
+
+    def wait_halo(copy, side, at, last):
+        @pl.when(at > 0 if side == 0 else at < last)
+        def _():
+            copy.wait_send()
+
+        @pl.when(at < last if side == 0 else at > 0)
+        def _():
+            copy.wait_recv()
 
     pairs = ((depth, h0), (bed, z0), (cells, m0), (mom_x, hu0), (mom_y, hv0))
 
@@ -336,7 +350,7 @@
         )
 
     for side in (0, 1):
-        halo_rows(row_snd1, row_rcv1, side, 0).start()
+        start_halo(halo_rows(row_snd1, row_rcv1, side, 0), side, gx, NGX - 1)
 
     cols1 = ([], [])
     for ref in (h0, hu0, hv0, m0, z0):
@@ -347,7 +361,18 @@
             cols1[side].append(ends[side])
     for side in (0, 1):
         col_snd1[side] = jnp.concatenate(cols1[side] + [jnp.zeros((3, ROWS), F32)], axis=0)
-        halo_cols(col_snd1, col_rcv1, side, 0).start()
+        start_halo(halo_cols(col_snd1, col_rcv1, side, 0), side, gy, NGY - 1)
+
+    load_small(5).wait()
+    cv = conv[...]
+    sec_lane = lax.broadcasted_iota(I32, (16, 512), 1)
+    face_k = jnp.where(sec_lane == 511, cv, 0.5 * (cv + pltpu.roll(cv, 511, 1)))
+    sewer_in[0] = heads[...]
+    sewer_in[1] = face_k
+    sewer_in[2] = jnp.where(sec_lane == 0, 0.0, pltpu.roll(face_k, 1, 1))
+    for l in range(16):
+        hit = jnp.broadcast_to(sec[l : l + 1] & 127, (128, 128)) == tile_iota
+        in_section[l] = hit.astype(F32).astype(BF16)
 
     row_iota = lax.broadcasted_iota(I32, (ROWS, 128), 0)
     for k in range(16):
@@ -427,11 +452,11 @@
         outs[1][ROWS] = part[1] - prev["h"] * sx_s[ROWS]
         outs[2][ROWS] = part[2]
 
-    sweep((h0, hu0, hv0), 0, (h1, hu1, hv1), None, 6, forward)
+    sweep((h0, hu0, hv0), 0, (h1, hu1, hv1), None, 8, forward)
 
     for side in (0, 1):
-        halo_rows(row_snd1, row_rcv1, side, 0).wait()
-        halo_cols(col_snd1, col_rcv1, side, 0).wait()
+        wait_halo(halo_rows(row_snd1, row_rcv1, side, 0), side, gx, NGX - 1)
+        wait_halo(halo_cols(col_snd1, col_rcv1, side, 0), side, gy, NGY - 1)
     exists_x = (gx > 0, gx < NGX - 1)
     exists_y = (gy > 0, gy < NGY - 1)
 
@@ -471,17 +496,6 @@
 
     lax.fori_loop(0, ROWS // 32, rolled_rows, 0)
 
-    load_small(5).wait()
-    cv = conv[...]
-    sec_lane = lax.broadcasted_iota(I32, (16, 512), 1)
-    face_k = jnp.where(sec_lane == 511, cv, 0.5 * (cv + pltpu.roll(cv, 511, 1)))
-    sewer_in[0] = heads[...]
-    sewer_in[1] = face_k
-    sewer_in[2] = jnp.where(sec_lane == 0, 0.0, pltpu.roll(face_k, 1, 1))
-    for l in range(16):
-        hit = jnp.broadcast_to(sec[l : l + 1] & 127, (128, 128)) == tile_iota
-        in_section[l] = hit.astype(F32).astype(BF16)
-
     pltpu.make_async_copy(got.at[pl.ds(0, NGY - 1)], got.at[pl.ds(0, NGY - 1)], p2_recv).wait()
     got_flat = got.reshape(NGX * NGY, 128)
     arrived = jnp.concatenate([got_flat[pl.ds(a, NGY, stride=NGX), :] for a in range(NGX)], axis=0).T
@@ -520,8 +534,8 @@
         own_y.append((cols2[0][side] - less, cols2[1][side], cols2[2][side]))
         col_snd2[side] = jnp.concatenate(list(own_y[side]) + [jnp.zeros((5, ROWS), F32)], axis=0)
     for side in (0, 1):
-        halo_rows(row_snd2, row_rcv2, side, 4).start()
-        halo_cols(col_snd2, col_rcv2, side, 4).start()
+        start_halo(halo_rows(row_snd2, row_rcv2, side, 4), side, gx, NGX - 1)
+        start_halo(halo_cols(col_snd2, col_rcv2, side, 4), side, gy, NGY - 1)
 
     level_sum = jnp.zeros((16, 128), F32)
     for k in range(16):
@@ -548,8 +562,8 @@
     sweep((h1, hu1, hv1), 1, (h2, hu2, hv2), (hur, hvr), 0, lambda: None)
 
     for side in (0, 1):
-        halo_rows(row_snd2, row_rcv2, side, 4).wait()
-        halo_cols(col_snd2, col_rcv2, side, 4).wait()
+        wait_halo(halo_rows(row_snd2, row_rcv2, side, 4), side, gx, NGX - 1)
+        wait_halo(halo_cols(col_snd2, col_rcv2, side, 4), side, gy, NGY - 1)
     halo_x = [[keep(exists_x[side], row_rcv2[side, f]) for f in range(3)] for side in (0, 1)]
     halo_y = [[keep(exists_y[side], col_rcv2[side, f : f + 1]) for f in range(3)] for side in (0, 1)]
     faces = faces_x(own_x, halo_x, hmx, hzx, mmx)

time: 24.4 us -> 23.9 us (0.980)
  Pallas kernels: 23.7 us -> 23 us
    pallas_call x1, Pallas kernels: 21.9 us -> 21.2 us  [body(): pl.pallas_call(kernel, out_shape=(padded,) * 3 + (pltpu.VMEM((2, 16, ROWS...]
where the time goes in v6:
time: 23.9 us; the launch traced here: 23.6 us
  Pallas kernels  23 us (96%)
  between operations  0.64 us (3%)
    pallas_call x1, Pallas kernels, body(): pl.pallas_call(kernel, out_shape=(padded,) * 3 + (pltpu.VMEM((2, 16, ROWS...  21.2 us
    pallas_call x1, Pallas kernels, body(): pl.pallas_call(finish, out_shape=(grid, grid, grid, sewer), in_specs=[vme...  1.77 us

profile of v6, /device:TPU:1, one launch (start us, length us, event | category | flops | bytes accessed | tf_op | source)
XLA Modules:
  0.0 23.6 jit_solution(17068878465741818543)
XLA Ops:
  0.6 21.2 %street_flood.1 = (f32[257,8,128]{2,1,0:T(8,128)S(1)}, f32[257,8,128]{2,1,0:T(8,128)S(1)}, f32[257,8,128]{2,1,0:T(8,128)S(1)}, f32[2,16,256]{2,1,0:T(8,128)S(1)}...) custom-call(f32[256,1024]{1,0:T(8,128)} %depth.1, f32[256,1024]{1,0:T(8,128)} %mom_x.1, f32[256,1024]{1,0:T(8,128)} %mom_y.1, ...), custom_call_target="tpu_custom_call" | custom-call | tf_op jit(solution)/shard_map/street_flood/pallas_call | solution.py:645
  21.9 1.8 %flood_finish.1 = (f32[256,1024]{1,0:T(8,128)}, f32[256,1024]{1,0:T(8,128)}, f32[256,1024]{1,0:T(8,128)}, f32[16,512]{1,0:T(8,128)}) custom-call(f32[257,8,128]{2,1,0:T(8,128)S(1)} %get-tuple-element.10.h2, f32[257,8,128]{2,1,0:T(8,128)S(1)} %get-tuple-element.11.hu2, f32[257,8,128]{2,1,0:T(8,128)S(1)} %get-tuple-element.12.hv2, ...), custom_call_target="tpu_custom_call" | custom-call | tf_op jit(solution)/shard_map/flood_finish/pallas_call | solution.py:694

commit v7 on v6

--- a/solution.py
+++ b/solution.py
@@ -452,7 +452,7 @@
         outs[1][ROWS] = part[1] - prev["h"] * sx_s[ROWS]
         outs[2][ROWS] = part[2]
 
-    sweep((h0, hu0, hv0), 0, (h1, hu1, hv1), None, 8, forward)
+    sweep((h0, hu0, hv0), 0, (h1, hu1, hv1), None, 10, forward)
 
     for side in (0, 1):
         wait_halo(halo_rows(row_snd1, row_rcv1, side, 0), side, gx, NGX - 1)

time: 23.9 us -> 24.1 us (level)
  Pallas kernels: 23 us -> 23.4 us
    pallas_call x1, Pallas kernels: 21.2 us -> 21.6 us  [body(): pl.pallas_call(kernel, out_shape=(padded,) * 3 + (pltpu.VMEM((2, 16, ROWS...]
where the time goes in v7:
time: 24.1 us; the launch traced here: 24 us
  Pallas kernels  23.4 us (97%)
  between operations  0.64 us (3%)
    pallas_call x1, Pallas kernels, body(): pl.pallas_call(kernel, out_shape=(padded,) * 3 + (pltpu.VMEM((2, 16, ROWS...  21.6 us
    pallas_call x1, Pallas kernels, body(): pl.pallas_call(finish, out_shape=(grid, grid, grid, sewer), in_specs=[vme...  1.77 us

profile of v7, /device:TPU:1, one launch (start us, length us, event | category | flops | bytes accessed | tf_op | source)
XLA Modules:
  0.0 24.0 jit_solution(14262233997857443124)
XLA Ops:
  0.6 21.6 %street_flood.1 = (f32[257,8,128]{2,1,0:T(8,128)S(1)}, f32[257,8,128]{2,1,0:T(8,128)S(1)}, f32[257,8,128]{2,1,0:T(8,128)S(1)}, f32[2,16,256]{2,1,0:T(8,128)S(1)}...) custom-call(f32[256,1024]{1,0:T(8,128)} %depth.1, f32[256,1024]{1,0:T(8,128)} %mom_x.1, f32[256,1024]{1,0:T(8,128)} %mom_y.1, ...), custom_call_target="tpu_custom_call" | custom-call | tf_op jit(solution)/shard_map/street_flood/pallas_call | solution.py:645
  22.3 1.8 %flood_finish.1 = (f32[256,1024]{1,0:T(8,128)}, f32[256,1024]{1,0:T(8,128)}, f32[256,1024]{1,0:T(8,128)}, f32[16,512]{1,0:T(8,128)}) custom-call(f32[257,8,128]{2,1,0:T(8,128)S(1)} %get-tuple-element.10.h2, f32[257,8,128]{2,1,0:T(8,128)S(1)} %get-tuple-element.11.hu2, f32[257,8,128]{2,1,0:T(8,128)S(1)} %get-tuple-element.12.hv2, ...), custom_call_target="tpu_custom_call" | custom-call | tf_op jit(solution)/shard_map/flood_finish/pallas_call | solution.py:694
